TPU v7x, 512 devices: a whole 4x4x16 slice. The times are simulated.
512 devices in a mesh: tm: 64 (over x, z), tok: 8 (over y, core).
Axes of the slice: x: 4, y: 4, z: 16, core: 2. Of those that a mesh axis runs over, the one named last changes fastest.
Arguments:
- anchor: float32 [4, 4, 1024], P(None, None, 'tok'), may hold values from -6 to 6
- latents: float32 [64, 4, 4, 1024], P('tm', None, None, 'tok'), may hold values from -6 to 6
- noise_draws: float32 [64, 4, 4, 1024], P('tm', None, None, 'tok'), may hold values from -6 to 6
- slot_steps: int32 [64, 2], P('tm'), may hold values from 0 to 999, as said below
- class_labels: int32 [4], replicated, may hold values from 0 to 999
- in_weight: bfloat16 [4, 1152], replicated, may hold values from -3 to 3
- time_weight: bfloat16 [256, 1152], replicated, may hold values from -0.375 to 0.375
- class_table: bfloat16 [1000, 1152], replicated, may hold values from -6 to 6
- mod_weight: bfloat16 [1152, 3456], P(None, 'tok'), may hold values from -0.09375 to 0.09375
- qkv_weight: bfloat16 [1152, 1728], P('tm'), may hold values from -0.25 to 0.25
- out_weight: bfloat16 [576, 1152], P('tm'), may hold values from -0.25 to 0.25
- final_weight: bfloat16 [4, 1152], replicated, may hold values from -0.1875 to 0.1875
Outputs:
- updated: float32 [64, 4, 4, 1024], P('tm', None, None, 'tok')
- errors: float32 [64, 4], P('tm')
Inputs may be any that keep to these rules, and one draw needn't show every extreme that they name: `slot_steps`: column 0 is the timestep a slot starts from, column 1 the one it steps to, smaller than column 0; each slot starts where the slot before it ends; slot 0 starts at 999 and the last slot steps to 0.
All inputs are finite; a program needn't handle non-finite values.
Results may differ from a plain program's by a relative error of at most 0.0025.
Values may be sent and summed in bfloat16 or wider, within the bound.
A program may use at most 128 MiB of HBM per device.

v0:
```python
import math

import jax
import jax.numpy as jnp
from jax import lax
from jax.sharding import PartitionSpec as P

D = 1152
HEAD = 72
HEADS = 8
CHAN = 4
CLASSES = 1000
FREQ = 256
SIDE = 32
TOKENS = 1024


def from_behind(value, axis, steps):
    count = lax.axis_size(axis)
    first, last = (max(0, -steps), min(count, count - steps))
    return lax.ppermute(value, axis, [(source, source + steps) for source in range(first, last)])


def entering(x, axis, combine, identity):
    peers, here = (lax.axis_size(axis), lax.axis_index(axis))
    everything = lax.all_gather(x, axis)
    start = jnp.broadcast_to(jnp.asarray(identity, x.dtype), x.shape)

    def hop(k, before):
        reached = k < here
        new = combine(before, everything[k])
        return jnp.where(reached, new, before)

    return lax.fori_loop(0, peers, hop, start)


def layer_norm(values):
    centered = values - jnp.mean(values, axis=-1, keepdims=True)
    variance = jnp.mean(centered * centered, axis=-1, keepdims=True)
    return centered * lax.rsqrt(variance + 1e-06)


def position_table(positions):
    quarter = D // 4
    angular = jnp.exp(-math.log(10000.0) * jnp.arange(quarter, dtype=jnp.float32) / quarter)
    row_pos = (positions // SIDE).astype(jnp.float32)[:, None] * angular[None, :]
    col_pos = (positions % SIDE).astype(jnp.float32)[:, None] * angular[None, :]
    return jnp.concatenate(
        [jnp.sin(row_pos), jnp.cos(row_pos), jnp.sin(col_pos), jnp.cos(col_pos)], axis=-1
    )


def time_features(t_from):
    half_freq = FREQ // 2
    angular = jnp.exp(-math.log(10000.0) * jnp.arange(half_freq, dtype=jnp.float32) / half_freq)
    phases = t_from * angular
    return jnp.concatenate([jnp.cos(phases), jnp.sin(phases)])[None, :]


def signal_level(step_value):
    return 0.005 + 0.99 * jnp.cos(0.4 * math.pi * step_value / 1000.0) ** 2


def coefficients(t_from, t_to):
    level_from = signal_level(t_from)
    level_to = signal_level(t_to)
    keep_coef = jnp.sqrt(level_to / level_from)
    noise_coef = (
        0.5
        * jnp.sqrt((1.0 - level_to) / (1.0 - level_from))
        * jnp.sqrt(1.0 - level_from / level_to)
    )
    eps_coef = jnp.sqrt(1.0 - level_to - noise_coef * noise_coef) - keep_coef * jnp.sqrt(
        1.0 - level_from
    )
    return (keep_coef, noise_coef, eps_coef)


def row_folder(left_rows, weight_rows):
    return jnp.dot(left_rows, weight_rows, preferred_element_type=jnp.float32)


def add_terms(earlier, later):
    return earlier + later


def project_local(normed_rows, qkv_weight, samples, local_len):
    qkv_all = row_folder(normed_rows, lax.all_gather(qkv_weight, "tm", axis=0, tiled=True))
    return qkv_all.astype(jnp.bfloat16).reshape(samples, local_len, 3, HEADS, HEAD)


def body(
    anchor,
    latents,
    noise_draws,
    slot_steps,
    class_labels,
    in_weight,
    time_weight,
    class_table,
    mod_weight,
    qkv_weight,
    out_weight,
    final_weight,
):
    samples = anchor.shape[0]
    local_len = anchor.shape[2]
    head_cols = HEADS * HEAD
    scale_factor = 1.0 / math.sqrt(HEAD)
    shifted = from_behind(latents, "tm", 1)
    slot_index = lax.axis_index("tm")
    prior = jnp.where(slot_index == 0, anchor, shifted[0])
    t_from = slot_steps[0, 0].astype(jnp.float32)
    t_to = slot_steps[0, 1].astype(jnp.float32)
    time_embed = jnp.dot(
        time_features(t_from), time_weight.astype(jnp.float32), precision=lax.Precision.HIGHEST
    )
    one_hot = (class_labels[:, None] == jnp.arange(CLASSES, dtype=jnp.int32)[None, :]).astype(
        jnp.bfloat16
    )
    class_embed = jnp.dot(one_hot, class_table, preferred_element_type=jnp.float32)
    condition_vec = jax.nn.silu(time_embed + class_embed).astype(jnp.bfloat16)
    mod_cols = jnp.dot(condition_vec, mod_weight, preferred_element_type=jnp.float32)
    modulation = lax.all_gather(mod_cols, "tok", axis=1, tiled=True)
    shift_m = modulation[:, :D]
    scale_m = modulation[:, D : 2 * D]
    gate_m = modulation[:, 2 * D :]
    positions = lax.axis_index("tok") * local_len + jnp.arange(local_len, dtype=jnp.int32)
    float_in = in_weight.astype(jnp.float32)
    embedded = (
        jnp.einsum("bcl,cd->bld", prior, float_in, precision=lax.Precision.HIGHEST)
        + position_table(positions)[None]
    )
    normed = (layer_norm(embedded) * (1.0 + scale_m[:, None]) + shift_m[:, None]).astype(
        jnp.bfloat16
    )
    normed_rows = normed.reshape(samples * local_len, D)
    qkv_all = project_local(normed_rows, qkv_weight, samples, local_len)
    queries = qkv_all[:, :, 0]
    key_rows = qkv_all[:, :, 1]
    value_rows = qkv_all[:, :, 2]
    key_part = lax.all_gather(key_rows, "tok", axis=1, tiled=True)
    value_part = lax.all_gather(value_rows, "tok", axis=1, tiled=True)
    scores = (
        jnp.einsum("bqhd,bkhd->bhqk", queries, key_part, preferred_element_type=jnp.float32)
        * scale_factor
    )
    exp_scores = jnp.exp(scores)
    totals = jnp.sum(exp_scores, axis=3)
    weighted = jnp.einsum(
        "bhqk,bkhd->bqhd",
        exp_scores.astype(jnp.bfloat16),
        value_part,
        preferred_element_type=jnp.float32,
    )
    weighted, totals = (weighted, totals)
    attended = (weighted / jnp.transpose(totals, (0, 2, 1))[..., None]).astype(jnp.bfloat16)
    attn_rows = attended.reshape(samples * local_len, head_cols)
    projected = row_folder(attn_rows, lax.all_gather(out_weight, "tm", axis=0, tiled=True))
    hidden_state = embedded + gate_m[:, None] * projected.reshape(samples, local_len, D)
    final_normed = layer_norm(hidden_state).astype(jnp.bfloat16)
    predicted = jnp.einsum(
        "bld,cd->bcl", final_normed, final_weight, preferred_element_type=jnp.float32
    )
    keep_coef, noise_coef, eps_coef = coefficients(t_from, t_to)
    drifts = ((keep_coef - 1.0) * prior + eps_coef * predicted + noise_coef * noise_draws[0])[None]
    earlier_sum = entering(drifts, "tm", add_terms, jnp.zeros_like(drifts))
    inclusive = earlier_sum + drifts
    updated = anchor[None] + inclusive
    change = updated - latents
    partial_value = jnp.sum(change * change, axis=(2, 3))
    summed = lax.psum(partial_value, "tok")
    errors = summed / (CHAN * TOKENS)
    return (updated, errors)


def solution(mesh):
    in_specs = (
        P(None, None, "tok"),
        P("tm", None, None, "tok"),
        P("tm", None, None, "tok"),
        P("tm", None),
        P(),
        P(),
        P(),
        P(),
        P(None, "tok"),
        P("tm", None),
        P("tm", None),
        P(),
    )
    out_specs = (P("tm", None, None, "tok"), P("tm", None))
    return jax.shard_map(body, mesh=mesh, in_specs=in_specs, out_specs=out_specs, check_vma=False)
```

profile of v0, /device:TPU:1, one launch (start us, length us, event | category | flops | bytes accessed | tf_op | source)
XLA Modules:
  0.0 536.3 jit_solution(4795089122641251004)
XLA Ops:
  7.2 0.7 all-gather.15.cloned.1.call-update
  8.0 5.0 collective-permute-start
  13.0 1.4 fusion.42
  15.1 1.4 convolution_reduce_fusion
  16.6 1.9 convolution_bitcast_fusion
  18.5 16.4 %all-gather.3 = f32[8,432,4]{1,2,0:T(4,128)S(1)} all-gather(f32[1,432,4]{1,2,0:T(4,128)S(1)} %convolution_bitcast_fusion), channel_id=1, replica_groups=mesh['tm'=64,'tok'=8] {'tok'}, dimensions={0}, use_global_device_ids=true | all-gather | bytes 62208 | tf_op jit(solution)/shard_map/all_gather | solution.py:124
  35.0 2.2 multiply_cosine_fusion
  37.2 1.2 concatenate.6
  38.5 2.2 fusion.43
  40.7 0.4 multiply_reduce_fusion.1
  41.0 1.0 copy-done.1
  42.0 0.8 add_convert_fusion
  42.9 115.3 %all-gather.15.cloned.1.call-done = bf16[64,18,1728]{2,1,0:T(8,128)(2,1)} async-done(((bf16[1,18,1728]{2,1,0:T(8,128)(2,1)}), bf16[64,18,1728]{2,1,0:T(8,128)(2,1)}) %all-gather.15.cloned.1.call-update) | async-done | bytes 3981328 | tf_op jit(solution)/shard_map/all_gather | solution.py:88
  158.1 7.7 %reshape.109 = bf16[1152,1728]{1,0:T(8,128)(2,1)} reshape(bf16[64,18,1728]{2,1,0:T(8,128)(2,1)} %all-gather.15.cloned.1.call-done) | data formatting | bytes 7962624
  165.8 5.9 %convolution_convert_fusion = bf16[512,1728]{0,1:T(8,128)(2,1)} fusion(bf16[512,1152]{1,0:T(8,128)(2,1)S(1)} %bitcast.86, bf16[1152,1728]{1,0:T(8,128)(2,1)} %reshape.109), kind=kOutput, calls=%fused_computation.12 | convolution fusion | flops 2039316480 | bytes 6930432 | tf_op jit(solution)/shard_map/dot_general | solution.py:80
  171.7 4.1 reshape.98
  175.9 2.0 fusion.40
  177.9 0.9 copy.31
  179.1 0.9 copy.29
  181.2 116.0 %all-gather.17.cloned.1.call-done = bf16[64,9,1152]{2,1,0:T(8,128)(2,1)} async-done(((bf16[1,9,1152]{2,1,0:T(8,128)(2,1)}), bf16[64,9,1152]{2,1,0:T(8,128)(2,1)}) %all-gather.17.cloned.1.call-update) | async-done | bytes 1327120 | tf_op jit(solution)/shard_map/all_gather | solution.py:159
  297.1 3.7 reshape.115
  300.8 49.2 %all-gather.13.cloned.1.call-done = bf16[4,1024,1,8,72]{1,4,3,0,2:T(8,128)(2,1)} async-done(((bf16[4,128,1,8,72]{1,4,3,0,2:T(8,128)(2,1)}), bf16[4,1024,1,8,72]{1,4,3,0,2:T(8,128)(2,1)}) %all-gather.13.cloned.1.call-update) | async-done | bytes 4718608 | tf_op jit(solution)/shard_map/all_gather | solution.py:142
  350.0 11.5 %fusion = (f32[4,8,128]{2,1,0:T(8,128)S(1)}, f32[4,8,128,1024]{3,2,1,0:T(8,128)}) fusion(bf16[4,1024,1,8,72]{1,4,3,0,2:T(8,128)(2,1)} %all-gather.13.cloned.1.call-done, bf16[4,128,1,8,72]{1,0,4,3,2:T(4,128)(2,1)S(1)} %get-tuple-element.120), kind=kOutput, calls=%fused_computation.2 | convolution fusion | flops 612364288 | bytes 22102016 | tf_op jit(solution)/shard_map/bqhd,bkhd->bhqk/dot_general | solution.py:145
  361.5 37.6 %all-gather.11.cloned.1.call-done = bf16[4,1024,1,8,72]{1,4,3,0,2:T(8,128)(2,1)} async-done(((bf16[4,128,1,8,72]{1,4,3,0,2:T(8,128)(2,1)}), bf16[4,1024,1,8,72]{1,4,3,0,2:T(8,128)(2,1)}) %all-gather.11.cloned.1.call-update) | async-done | bytes 4718608 | tf_op jit(solution)/shard_map/all_gather | solution.py:143
  399.0 10.2 %divide_convert_fusion = bf16[4,128,8,72]{1,3,2,0:T(8,128)(2,1)S(1)} fusion(f32[4,8,128,1024]{3,2,1,0:T(8,128)} %get-tuple-element.136, bf16[4,1024,1,8,72]{1,4,3,0,2:T(8,128)(2,1)} %all-gather.11.cloned.1.call-done, f32[4,128,8]{1,2,0:T(8,128)S(1)} %bitcast.90), kind=kOutput, calls=%fused_computation.22 | convolution fusion | flops 612958208 | bytes 22102016 | tf_op jit(solution)/shard_map/bhqk,bkhd->bqhd/dot_general | solution.py:150
  409.3 1.3 fusion.44
  411.4 1.3 bitcast_add_fusion.1
  412.6 76.4 %all-gather.2 = f32[256,4,128]{2,1,0:T(4,128)S(1)} all-gather(f32[4,4,128]{2,1,0:T(4,128)S(1)} %bitcast_add_fusion.1), channel_id=4, replica_groups=mesh['tm'=64,'tok'=8] {'tm'}, dimensions={0}, use_global_device_ids=true | all-gather | bytes 532480 | tf_op jit(solution)/shard_map/all_gather | solution.py:26
  489.0 2.6 while.14
  491.6 0.6 multiply_reduce_fusion.2
  492.2 37.0 %psum.7 = f32[1,4]{1,0:T(1,128)S(1)} all-reduce(f32[1,4]{1,0:T(1,128)S(1)} %bitcast.93), channel_id=1, replica_groups=mesh['tm'=64,'tok'=8] {'tok'}, use_global_device_ids=true, to_apply=%region_8.9 | all-reduce | flops 4 | bytes 32 | tf_op jit(solution)/shard_map/psum | solution.py:172
  529.3 0.5 broadcast_multiply_fusion.2
  (100 shorter events, 2.4 us)
Async XLA Ops:
  7.2 9.4 %copy-start = (bf16[1000,1152]{1,0:T(8,128)(2,1)S(1)}, bf16[1000,1152]{1,0:T(8,128)(2,1)}, u32[]{:S(2)}) copy-start(bf16[1000,1152]{1,0:T(8,128)(2,1)} %param.21) | copy-start | bytes 6912004
  7.2 150.9 %all-gather.15.cloned.1.call-start = ((), (), s32[]{:S(2)}) async-start(), calls=%async_computation.2 | async-start | bytes 5591040 | tf_op jit(solution)/shard_map/all_gather | solution.py:88
  7.9 289.2 %all-gather.17.cloned.1.call-start = ((), (), s32[]{:S(2)}) async-start(), calls=%async_computation.3 | async-start | bytes 2396160 | tf_op jit(solution)/shard_map/all_gather | solution.py:159
  8.0 30.5 %collective-permute-start = (f32[1,4,4,128]{3,2,1,0:T(4,128)}, f32[1,4,4,128]{3,2,1,0:T(4,128)}, u32[]{:S(2)}, u32[]{:S(2)}) collective-permute-start(f32[1,4,4,128]{3,2,1,0:T(4,128)} %param.15), channel_id=1, source_target_pairs={{0,8},{8,16},{16,24},{24,32},{32,40},{40,48},{48,56},{56,64},{64,7... | collective-permute-start | bytes 24584 | tf_op jit(solution)/shard_map/ppermute | solution.py:21
  12.9 337.1 %all-gather.13.cloned.1.call-start = ((), (), s32[]{:S(2)}) async-start(), calls=%async_computation.1 | async-start | bytes 5308416 | tf_op jit(solution)/shard_map/all_gather | solution.py:142
  16.6 21.9 %copy-start.4 = (f32[4,4,128]{2,1,0:T(4,128)S(1)}, f32[4,4,128]{2,1,0:T(4,128)}, u32[]{:S(2)}) copy-start(f32[4,4,128]{2,1,0:T(4,128)} %param.14) | copy-start | bytes 24580
  40.6 1.4 copy-start.1
  178.8 220.2 %all-gather.11.cloned.1.call-start = ((), (), s32[]{:S(2)}) async-start(), calls=%async_computation | async-start | bytes 5308416 | tf_op jit(solution)/shard_map/all_gather | solution.py:143
  399.0 10.2 %copy-start.2 = (f32[4,128,1152]{2,1,0:T(8,128)S(1)}, f32[4,128,1152]{2,1,0:T(8,128)}, u32[]{:S(2)}) copy-start(f32[4,128,1152]{2,1,0:T(8,128)} %copy-done.1) | copy-start | bytes 7077892
  399.0 10.3 %copy-start.3 = (bf16[576,1152,1]{1,0,2:T(8,128)(2,1)S(1)}, bf16[576,1152,1]{1,0,2:T(8,128)(2,1)}, u32[]{:S(2)}) copy-start(bf16[576,1152,1]{1,0,2:T(8,128)(2,1)} %reshape.115) | copy-start | bytes 3981316
  410.6 0.7 copy-start.5
  410.6 0.7 copy-start.6
  410.7 80.9 %copy-start.7 = (f32[1,4,4,128]{3,2,1,0:T(4,128)S(1)}, f32[1,4,4,128]{3,2,1,0:T(4,128)}, u32[]{:S(2)}) copy-start(f32[1,4,4,128]{3,2,1,0:T(4,128)} %param.15) | copy-start | bytes 24580
Sparse Core Ops, SparseCore 0:
  11.0 147.1 all-gather.14
  161.1 135.9 all-gather.16
  299.2 50.7 all-gather.12
  352.0 47.0 all-gather.10
where the time goes:
time: 537 us; the launch traced here: 536 us
  waiting for transfers between devices  319 us (59%)
  blocking collectives  130 us (24%)
  matrix products  35.7 us (7%)
  local copies, waits for them, and re-layouts  23.5 us (4%)
  between operations  15.8 us (3%)
  other arithmetic  6.02 us (1%)
    all_gather x1, waiting for transfers between devices, body(): lax.all_gather(out_weight, 'tm', axis=0, tiled=True)  116 us
    all_gather x1, waiting for transfers between devices, project_local(): lax.all_gather(qkv_weight, 'tm', axis=0, tiled=True)  115 us
    all_gather x1, blocking collectives, entering(): everything = lax.all_gather(x, axis)  76.4 us
    all_gather x1, waiting for transfers between devices, body(): key_part = lax.all_gather(key_rows, 'tok', axis=1, tiled=True)  49.2 us
    all_gather x1, waiting for transfers between devices, body(): value_part = lax.all_gather(value_rows, 'tok', axis=1, tiled=True)  37.6 us
    psum x1, blocking collectives, body(): summed = lax.psum(partial_value, 'tok')  37 us
    all_gather x1, blocking collectives, body(): modulation = lax.all_gather(mod_cols, 'tok', axis=1, tiled=True)  16.4 us
    unnamed x21, local copies, waits for them, and re-layouts  14.7 us
  transfers between devices with their start and end apart: 5, of which 4 were waited for; matrix products, arithmetic and copies ran while one was open for 9% of the time, Pallas kernels for 0%

commit v1 on v0

v1 whole, which is shorter than its diff:
```python
import math

import jax
import jax.numpy as jnp
import ml_dtypes
import numpy as np
from jax import lax
from jax.experimental import pallas as pl
from jax.experimental.pallas import tpu as pltpu
from jax.sharding import PartitionSpec as P

MESH = pl.DeviceIdType.MESH
D = 1152
HEAD = 72
HEADS = 8
CHAN = 4
FREQ = 256
SIDE = 32
TOKENS = 1024
IMAGES = 4
NX, NZ, NT = 4, 16, 8
SLOTS = NX * NZ
HP = 80
POSK = 6 * SIDE
KX = POSK + 16
HALF = 512
F32 = jnp.float32
BF16 = jnp.bfloat16


def split3(values):
    high = values.astype(BF16).astype(F32)
    rest = values - high
    mid = rest.astype(BF16).astype(F32)
    return high, mid, rest - mid


def position_constants():
    quarter = D // 4
    angular = np.exp(np.float32(-math.log(10000.0)) * np.arange(quarter, dtype=np.float32) / np.float32(quarter)).astype(np.float32)
    angles = (np.arange(SIDE, dtype=np.float32)[:, None] * angular[None, :]).astype(np.float32)
    pair = np.concatenate([np.sin(angles), np.cos(angles)], axis=1).astype(np.float32)
    table = np.zeros((D, POSK), dtype=ml_dtypes.bfloat16)
    rest = pair
    for part in range(3):
        term = rest.astype(ml_dtypes.bfloat16)
        rest = rest - term.astype(np.float32)
        table[: D // 2, part * SIDE : (part + 1) * SIDE] = term.T
        table[D // 2 :, (3 + part) * SIDE : (4 + part) * SIDE] = term.T
    tokens = np.arange(TOKENS)
    select = np.zeros((POSK, TOKENS), dtype=ml_dtypes.bfloat16)
    for part in range(3):
        select[part * SIDE + tokens // SIDE, tokens] = 1
        select[(3 + part) * SIDE + tokens % SIDE, tokens] = 1
    return table, select


def kernel(
    coef_ref, lat_ref, anchor_ref, noise_ref, feat_ref, cls_ref, fw_ref,
    wmain_ref, wrem_ref, wo_ref, time_hbm, mod_hbm, table_hbm, select_hbm,
    upd_ref, err_ref,
    time_w, mod_w, table, xs, psrc, pr, mod_s, mod_r, mod_t, bc,
    zw, zr, wf, wx, wt, zo, of, wob, emb, own, normed, att_s, att_r,
    dr_r, tx_r, er_r, er_s,
    loc_sem, pr_send, pr_recv, mod_send, mod_recv, zw_send, zw_recv, zr_send, zr_recv,
    wx_send, wx_recv, zo_send, zo_recv, ox_send, ox_recv, sib_send, sib_recv,
    att_send, att_recv, dr_send, dr_recv, tx_send, tx_recv, er_send, er_recv,
):
    slot = lax.axis_index("tm")
    tok = lax.axis_index("tok")
    x = lax.div(slot, NZ)
    z = lax.rem(slot, NZ)
    core = lax.rem(tok, 2)
    sibling = tok + 1 - 2 * core

    def z_peer(k):
        return (x * NZ + lax.rem(z + k, NZ), tok)

    def x_peer(k):
        return (lax.rem(x + k, NX) * NZ + z, tok)

    def t_peer(k):
        return (slot, lax.rem(tok + k, NT))

    def each(count, action, first=1):
        def step(k, carry):
            action(k)
            return carry

        lax.fori_loop(first, count, step, 0)

    def remote(src, dst, send, recv, device):
        return pltpu.make_async_remote_copy(
            src_ref=src, dst_ref=dst, send_sem=send, recv_sem=recv, device_id=device, device_id_type=MESH
        )

    loads = [
        pltpu.make_async_copy(time_hbm, time_w, loc_sem.at[0]),
        pltpu.make_async_copy(mod_hbm, mod_w, loc_sem.at[1]),
        pltpu.make_async_copy(table_hbm, table, loc_sem.at[2]),
        pltpu.make_async_copy(select_hbm, xs.at[pl.ds(0, POSK)], loc_sem.at[3]),
    ]
    for load in loads:
        load.start()

    barrier = pltpu.get_barrier_semaphore()

    def greet(device):
        pl.semaphore_signal(barrier, inc=1, device_id=device, device_id_type=MESH)

    each(NZ, lambda k: greet(z_peer(k)))
    each(NX, lambda k: greet(x_peer(k)))
    each(NT, lambda k: greet(t_peer(k)))
    before = lax.rem(slot + SLOTS - 1, SLOTS)
    after = lax.rem(slot + 1, SLOTS)
    each(NT, lambda k: greet((before, k)), first=0)
    psrc[...] = jnp.where(slot == SLOTS - 1, anchor_ref[...], lat_ref[0])
    zw[z] = wmain_ref[...]
    zr[z] = wrem_ref[...]
    zo[z] = wo_ref[...]
    pl.semaphore_wait(barrier, NZ - 1 + NX - 1 + NT - 1 + NT)

    def prior_copy(k):
        return remote(psrc, pr.at[tok], pr_send.at[k], pr_recv.at[tok], (after, k))

    def prior_arrival(k):
        return remote(psrc, pr.at[k], pr_send.at[k], pr_recv.at[k], (after, k))

    def zw_copy(k):
        return remote(zw.at[z], zw.at[z], zw_send.at[k], zw_recv.at[k], z_peer(k))

    def zr_copy(k):
        return remote(zr.at[z], zr.at[z], zr_send.at[k], zr_recv.at[k], z_peer(k))

    def zo_copy(k):
        return remote(zo.at[z], zo.at[z], zo_send.at[k], zo_recv.at[k], z_peer(k))

    def wx_copy(k):
        return remote(wx.at[x], wx.at[x], wx_send.at[k], wx_recv.at[k], x_peer(k))

    def ox_copy(k):
        return remote(wob.at[core, x], wob.at[core, x], ox_send.at[k], ox_recv.at[k], x_peer(k))

    def mod_copy(k):
        return remote(mod_s, mod_r.at[tok], mod_send.at[k], mod_recv.at[k], t_peer(k))

    def att_copy(b, k):
        there = lax.rem(tok + k, NT)
        return remote(att_s.at[b, there], att_r.at[b, tok], att_send.at[b, k], att_recv.at[b, k], t_peer(k))

    each(NT, lambda k: prior_copy(k).start(), first=0)

    def start_w(k):
        zw_copy(k).start()
        zr_copy(k).start()

    each(NZ, start_w)

    loads[0].wait()
    high, mid, low = split3(feat_ref[...])
    feats = jnp.concatenate([high, mid, low, jnp.zeros((5, FREQ), F32)], axis=0).astype(BF16)
    parts = jnp.dot(feats, time_w[...], preferred_element_type=F32)
    value = parts[0:1] + parts[1:2] + parts[2:3] + cls_ref[...]
    condition = (value / (1.0 + jnp.exp(-value))).astype(BF16)
    loads[1].wait()
    mod_s[:, 432:512] = jnp.zeros((8, 80), F32)
    mod_s[:, 0:432] = jnp.dot(condition, mod_w[...], preferred_element_type=F32)
    mod_r[tok] = mod_s[...]
    each(NT, lambda k: mod_copy(k).start())
    loads[2].wait()
    loads[3].wait()
    each(NT, lambda k: mod_copy(k).wait())
    for source in range(NT):
        mod_t[source * 432 : source * 432 + 432] = jnp.transpose(mod_r[source])[0:432]
    for b in range(IMAGES):
        bc[b, 0] = jnp.broadcast_to(1.0 + mod_t[D : 2 * D, b : b + 1], (D, 128))
        bc[b, 1] = jnp.broadcast_to(mod_t[0:D, b : b + 1], (D, 128))
    each(NT, lambda k: prior_arrival(k).wait(), first=0)

    rows = 48

    def embed(step, carry):
        b, part = lax.div(step, 2), lax.rem(step, 2)
        line = jnp.concatenate([pr[4 * part + t, b] for t in range(4)], axis=1)
        high, mid, low = split3(line)
        split = jnp.concatenate([high, mid, low, jnp.zeros((4, HALF), F32)], axis=0)
        lanes = pl.ds(pl.multiple_of(part * HALF, HALF), HALF)
        xs[POSK:KX, lanes] = split.astype(BF16)
        emb[...] = jnp.dot(table[...], xs[:, lanes], preferred_element_type=F32)

        def add(r, total):
            chunk = emb[pl.ds(pl.multiple_of(r * rows, rows), rows)]
            return total + jnp.sum(chunk.reshape(rows // 8, 8, HALF), axis=0)

        total = lax.fori_loop(0, D // rows, add, jnp.zeros((8, HALF), F32))
        mean = jnp.sum(total, axis=0, keepdims=True) * (1.0 / D)

        def square(r, total):
            chunk = emb[pl.ds(pl.multiple_of(r * rows, rows), rows)] - mean
            return total + jnp.sum((chunk * chunk).reshape(rows // 8, 8, HALF), axis=0)

        total = lax.fori_loop(0, D // rows, square, jnp.zeros((8, HALF), F32))
        inverse = lax.rsqrt(jnp.sum(total, axis=0, keepdims=True) * (1.0 / D) + 1e-06)

        def scale(r, carry):
            here = pl.ds(pl.multiple_of(r * rows, rows), rows)
            gain, shift = bc[b, 0, here], bc[b, 1, here]
            for t in range(4):
                cut = slice(t * 128, t * 128 + 128)
                out = (emb[here, cut] - mean[:, cut]) * inverse[:, cut] * gain + shift
                normed[b, here, pl.ds(pl.multiple_of(part * HALF + t * 128, 128), 128)] = out.astype(BF16)
            return carry

        lax.fori_loop(0, D // rows, scale, 0)

        @pl.when(part == lax.div(tok, 4))
        def _():
            mine = pl.ds(pl.multiple_of(lax.rem(tok, 4) * 128, 128), 128)
            own[b] = emb[:, mine]

        return carry

    lax.fori_loop(0, 4, embed, 0)

    def arrive_w(k):
        zw_copy(k).wait()
        zr_copy(k).wait()

    each(NZ, arrive_w)
    each(NZ, lambda k: zo_copy(k).start())
    for i in range(NZ):
        wf[18 * i : 18 * i + 16] = zw[i].astype(F32)
        wf[18 * i + 16 : 18 * i + 18] = zr[i]
    wx[x] = wf[...].astype(BF16)
    each(NX, lambda k: wx_copy(k).start())
    lax.fori_loop(4, 8, embed, 0)
    each(NX, lambda k: wx_copy(k).wait())
    wt[...] = jnp.transpose(wx[...].reshape(D, 256))

    factor = math.log2(math.e) / math.sqrt(HEAD)
    block = 256

    def attend(b, carry):
        qkv = jnp.dot(wt[...], normed[b], preferred_element_type=F32)
        queries = qkv[0:HEAD].astype(BF16)
        keys = qkv[HEAD : 2 * HEAD].astype(BF16)
        values = jnp.concatenate([qkv[2 * HEAD : 3 * HEAD], jnp.ones((8, TOKENS), F32)], axis=0).astype(BF16)
        for i in range(TOKENS // block):
            scores = lax.dot_general(
                keys, queries[:, i * block : (i + 1) * block], (((0,), (0,)), ((), ())), preferred_element_type=F32
            )
            weights = jnp.exp2(scores * factor).astype(BF16)
            summed = jnp.dot(values, weights, preferred_element_type=F32)
            out = (summed / summed[HEAD : HEAD + 1]).astype(BF16)
            for t in range(2):
                att_s[b, 2 * i + t] = out[:, t * 128 : t * 128 + 128]
        att_r[b, tok] = att_s[b, tok]
        each(NT, lambda k: att_copy(b, k).start())
        return carry

    lax.fori_loop(0, 2, attend, 0)

    each(NZ, lambda k: zo_copy(k).wait())
    for i in range(NZ):
        base = 9 * i + (HP - HEAD) * (i // 8)
        of[base : base + 9] = zo[i].astype(F32)[0:9]
    for h in range(2):
        of[h * HP + HEAD : (h + 1) * HP] = jnp.zeros((HP - HEAD, 640), F32)
    wob[core, x] = of[...].astype(BF16)
    each(NX, lambda k: ox_copy(k).start())
    lax.fori_loop(2, 4, attend, 0)
    each(NX, lambda k: ox_copy(k).wait())
    share = remote(wob.at[core], wob.at[core], sib_send, sib_recv, (slot, sibling))
    share.start()
    other = remote(wob.at[1 - core], wob.at[1 - core], sib_send, sib_recv, (slot, sibling))
    each(NT, lambda k: [att_copy(b, k).wait() for b in range(IMAGES)])
    share.wait_send()
    other.wait_recv()

    attended = jnp.concatenate([att_r[b].reshape(HEADS * HP, 128) for b in range(IMAGES)], axis=1)
    contract = (((0,), (0,)), ((), ()))
    emb[0:640] = lax.dot_general(wob[0].reshape(HEADS * HP, 640), attended, contract, preferred_element_type=F32)
    emb[640:D] = lax.dot_general(wob[1].reshape(HEADS * HP, 640)[:, 128:640], attended, contract, preferred_element_type=F32)

    def hidden(r, total):
        here = pl.ds(pl.multiple_of(r * rows, rows), rows)
        gates = mod_t[pl.ds(pl.multiple_of(2 * D + r * rows, rows), rows)]
        sums = []
        for b in range(IMAGES):
            cut = slice(b * 128, b * 128 + 128)
            value = own[b, here] + gates[:, b : b + 1] * emb[here, cut]
            emb[here, cut] = value
            sums.append(jnp.sum(value.reshape(rows // 8, 8, 128), axis=0))
        return total + jnp.concatenate(sums, axis=1)

    total = lax.fori_loop(0, D // rows, hidden, jnp.zeros((8, HALF), F32))
    mean = jnp.sum(total, axis=0, keepdims=True) * (1.0 / D)

    def square(r, total):
        chunk = emb[pl.ds(pl.multiple_of(r * rows, rows), rows)] - mean
        return total + jnp.sum((chunk * chunk).reshape(rows // 8, 8, HALF), axis=0)

    total = lax.fori_loop(0, D // rows, square, jnp.zeros((8, HALF), F32))
    inverse = lax.rsqrt(jnp.sum(total, axis=0, keepdims=True) * (1.0 / D) + 1e-06)
    final = ((emb[...] - mean) * inverse).astype(BF16)
    predicted = jnp.dot(fw_ref[...], final, preferred_element_type=F32)

    keep, eps, noise = coef_ref[0], coef_ref[1], coef_ref[2]
    for b in range(IMAGES):
        dr_r[z, b] = keep * pr[tok, b] + eps * predicted[0:CHAN, b * 128 : b * 128 + 128] + noise * noise_ref[0, b]

    def dr_copy(k):
        return remote(dr_r.at[z], dr_r.at[z], dr_send.at[k], dr_recv.at[k], z_peer(k))

    def tx_copy(k):
        return remote(tx_r.at[x], tx_r.at[x], tx_send.at[k], tx_recv.at[k], x_peer(k))

    each(NZ, lambda k: dr_copy(k).start())
    each(NZ, lambda k: dr_copy(k).wait())
    nothing = jnp.zeros((IMAGES, CHAN, 128), F32)
    whole, reached = nothing, nothing
    for i in range(NZ):
        term = dr_r[i]
        whole = whole + term
        reached = reached + jnp.where(i <= z, term, nothing)
    tx_r[x] = whole
    each(NX, lambda k: tx_copy(k).start())
    each(NX, lambda k: tx_copy(k).wait())
    earlier = nothing
    for i in range(NX):
        earlier = earlier + jnp.where(i < x, tx_r[i], nothing)
    updated = anchor_ref[...] + (earlier + reached)
    upd_ref[0] = updated
    change = updated - lat_ref[0]
    er_s[...] = jnp.sum(change * change, axis=1)
    er_r[tok] = er_s[...]

    def er_copy(k):
        return remote(er_s, er_r.at[tok], er_send.at[k], er_recv.at[k], t_peer(k))

    each(NT, lambda k: er_copy(k).start())
    each(NT, lambda k: er_copy(k).wait())
    err_ref[...] = jnp.sum(jnp.sum(er_r[...], axis=0), axis=1, keepdims=True) * (1.0 / (CHAN * TOKENS))


def time_features(t_from):
    half_freq = FREQ // 2
    angular = jnp.exp(-math.log(10000.0) * jnp.arange(half_freq, dtype=F32) / half_freq)
    phases = t_from * angular
    return jnp.concatenate([jnp.cos(phases), jnp.sin(phases)])[None, :]


def signal_level(step_value):
    return 0.005 + 0.99 * jnp.cos(0.4 * math.pi * step_value / 1000.0) ** 2


def coefficients(t_from, t_to):
    level_from = signal_level(t_from)
    level_to = signal_level(t_to)
    keep_coef = jnp.sqrt(level_to / level_from)
    noise_coef = 0.5 * jnp.sqrt((1.0 - level_to) / (1.0 - level_from)) * jnp.sqrt(1.0 - level_from / level_to)
    eps_coef = jnp.sqrt(1.0 - level_to - noise_coef * noise_coef) - keep_coef * jnp.sqrt(1.0 - level_from)
    return (keep_coef, noise_coef, eps_coef)


def body(
    anchor, latents, noise_draws, slot_steps, class_labels, in_weight, time_weight, class_table,
    mod_weight, qkv_weight, out_weight, final_weight,
):
    tok = lax.axis_index("tok")
    t_from = slot_steps[0, 0].astype(F32)
    t_to = slot_steps[0, 1].astype(F32)
    keep_coef, noise_coef, eps_coef = coefficients(t_from, t_to)
    coef = jnp.stack([keep_coef - 1.0, eps_coef, noise_coef])
    features = time_features(t_from)
    classes = jnp.concatenate(
        [lax.dynamic_slice(class_table, (class_labels[b], 0), (1, D)) for b in range(IMAGES)]
        + [jnp.zeros((4, D), BF16)],
        axis=0,
    ).astype(F32)
    head_cols = jnp.concatenate(
        [lax.dynamic_slice(qkv_weight, (0, HEAD * (HEADS * i + tok)), (18, HEAD)) for i in range(3)]
        + [jnp.zeros((18, 40), BF16)],
        axis=1,
    )
    w_main = head_cols[:16]
    w_rem = head_cols[16:].astype(F32)
    wo = jnp.pad(lax.dynamic_slice(out_weight, (0, 512 * lax.rem(tok, 2)), (9, 640)), ((0, 7), (0, 0)))
    table, select = position_constants()
    turned = in_weight.T
    table = jnp.concatenate(
        [jnp.asarray(table), turned, turned, turned, jnp.zeros((D, 4), BF16)], axis=1
    )
    vmem = pl.BlockSpec(memory_space=pltpu.VMEM)
    anywhere = pl.BlockSpec(memory_space=pl.ANY)
    dma = pltpu.SemaphoreType.DMA
    updated, errors = pl.pallas_call(
        kernel,
        out_shape=(
            jax.ShapeDtypeStruct((1, IMAGES, CHAN, 128), F32),
            jax.ShapeDtypeStruct((IMAGES, 1), F32),
        ),
        in_specs=[pl.BlockSpec(memory_space=pltpu.SMEM)] + [vmem] * 9 + [anywhere] * 4,
        out_specs=(vmem, vmem),
        scratch_shapes=[
            pltpu.VMEM((FREQ, D), BF16),
            pltpu.VMEM((D, 432), BF16),
            pltpu.VMEM((D, KX), BF16),
            pltpu.VMEM((KX, TOKENS), BF16),
            pltpu.VMEM((IMAGES, CHAN, 128), F32),
            pltpu.VMEM((NT, IMAGES, CHAN, 128), F32),
            pltpu.VMEM((8, 512), F32),
            pltpu.VMEM((NT, 8, 512), F32),
            pltpu.VMEM((3 * D, 8), F32),
            pltpu.VMEM((IMAGES, 2, D, 128), F32),
            pltpu.VMEM((NZ, 16, 256), BF16),
            pltpu.VMEM((NZ, 2, 256), F32),
            pltpu.VMEM((18 * NZ, 256), F32),
            pltpu.VMEM((NX, 18 * NZ, 256), BF16),
            pltpu.VMEM((256, D), BF16),
            pltpu.VMEM((NZ, 16, 640), BF16),
            pltpu.VMEM((2 * HP, 640), F32),
            pltpu.VMEM((2, NX, 2 * HP, 640), BF16),
            pltpu.VMEM((D, HALF), F32),
            pltpu.VMEM((IMAGES, D, 128), F32),
            pltpu.VMEM((IMAGES, D, TOKENS), BF16),
            pltpu.VMEM((IMAGES, NT, HP, 128), BF16),
            pltpu.VMEM((IMAGES, NT, HP, 128), BF16),
            pltpu.VMEM((NZ, IMAGES, CHAN, 128), F32),
            pltpu.VMEM((NX, IMAGES, CHAN, 128), F32),
            pltpu.VMEM((NT, IMAGES, 128), F32),
            pltpu.VMEM((IMAGES, 128), F32),
            dma((4,)),
            dma((NT,)), dma((NT,)),
            dma((NT,)), dma((NT,)),
            dma((NZ,)), dma((NZ,)),
            dma((NZ,)), dma((NZ,)),
            dma((NX,)), dma((NX,)),
            dma((NZ,)), dma((NZ,)),
            dma((NX,)), dma((NX,)),
            dma, dma,
            dma((IMAGES, NT)), dma((IMAGES, NT)),
            dma((NZ,)), dma((NZ,)),
            dma((NX,)), dma((NX,)),
            dma((NT,)), dma((NT,)),
        ],
        compiler_params=pltpu.CompilerParams(
            collective_id=0, has_side_effects=True, vmem_limit_bytes=56 * 1024 * 1024
        ),
        cost_estimate=pl.CostEstimate(flops=6_000_000_000, bytes_accessed=8_000_000, transcendentals=4_200_000),
    )(
        coef, latents, anchor, noise_draws, features, classes, final_weight,
        w_main, w_rem, wo, time_weight, mod_weight, table, jnp.asarray(select),
    )
    return updated, errors.reshape(1, IMAGES)


def solution(mesh):
    in_specs = (
        P(None, None, "tok"),
        P("tm", None, None, "tok"),
        P("tm", None, None, "tok"),
        P("tm", None),
        P(),
        P(),
        P(),
        P(),
        P(None, "tok"),
        P("tm", None),
        P("tm", None),
        P(),
    )
    out_specs = (P("tm", None, None, "tok"), P("tm", None))
    return jax.shard_map(body, mesh=mesh, in_specs=in_specs, out_specs=out_specs, check_vma=False)
```

time: 537 us -> 120 us (0.22)
  waiting for transfers between devices: 319 us -> 0 us
  blocking collectives: 130 us -> 0 us
  Pallas kernels: 0 us -> 92.8 us
  matrix products: 35.7 us -> 0 us
  local copies, waits for them, and re-layouts: 23.5 us -> 12.7 us
  between operations: 15.8 us -> 10.1 us
    all_gather x4 -> x0, waiting for transfers between devices: 318 us -> none  [the longest x1 116 us: body(): lax.all_gather(out_weight, 'tm', axis=0, tiled=True)]
    pallas_call x0 -> x1, Pallas kernels: none -> 92.8 us  [body(): pl.pallas_call(kernel, out_shape=(jax.ShapeDtypeStruct((1, IMAGES, CHAN,...]
    all_gather x2 -> x0, blocking collectives: 92.7 us -> none  [the longest x1 76.4 us: entering(): everything = lax.all_gather(x, axis)]
    psum x1 -> x0, blocking collectives: 37 us -> none  [body(): summed = lax.psum(partial_value, 'tok')]
    dot_general x8 -> x0, matrix products: 35.7 us -> none  [the longest x1 11.5 us: body(): jnp.einsum('bqhd,bkhd->bhqk', queries, key_part, preferred_element_type=j...]
    unnamed x21 -> x7, local copies, waits for them, and re-layouts: 14.7 us -> 3.87 us
  transfers between devices with their start and end apart: 5 -> 0, of which waited for: 4 -> 0; matrix products, arithmetic and copies ran while one was open for 9% -> 0% of each run, Pallas kernels for 0% -> 0%
where the time goes in v1:
time: 120 us; the launch traced here: 119 us
  Pallas kernels  92.8 us (77%)
  local copies, waits for them, and re-layouts  12.7 us (11%)
  between operations  10.1 us (8%)
  other arithmetic  3.85 us (3%)
    pallas_call x1, Pallas kernels, body(): pl.pallas_call(kernel, out_shape=(jax.ShapeDtypeStruct((1, IMAGES, CHAN,...  92.8 us
    unnamed x7, local copies, waits for them, and re-layouts  3.87 us
    concatenate x1, local copies, waits for them, and re-layouts, body(): jnp.concatenate([jnp.asarray(table), turned, turned, turned, jnp.zeros((D...  3.02 us

profile of v1, /device:TPU:1, one launch (start us, length us, event | category | flops | bytes accessed | tf_op | source)
XLA Modules:
  0.0 119.5 jit_solution(14455871994538130552)
XLA Ops:
  0.6 0.0 copy-start
  0.6 0.0 copy-start.1
  0.7 0.1 pad.8.clone
  0.8 1.3 %fusion.3 = (s32[1,1]{1,0:T(1,128)}, s32[1,1]{1,0:T(1,128)}) fusion(s32[1,2]{1,0:T(1,128)} %param.17), kind=kLoop, calls=%fused_computation.16 | loop fusion | bytes 16 | tf_op jit(solution)/shard_map/slice | solution.py:371
  3.9 0.7 pad_maximum_fusion.1.coef_ref
  4.6 0.6 pad_maximum_fusion
  5.1 1.5 %fusion.2 = (s32[1]{0:T(128)}, s32[1]{0:T(128)}, s32[1]{0:T(128)}, s32[1]{0:T(128)}) fusion(s32[4]{0:T(128)} %param.18), kind=kLoop, calls=%fused_computation.15 | loop fusion | bytes 32 | tf_op jit(solution)/shard_map/slice | solution.py:377
  14.2 0.8 constant_dynamic-slice_fusion.4
  15.1 0.1 concatenate.13
  15.1 0.8 constant_dynamic-slice_fusion.3
  15.9 0.1 maximum_maximum_fusion
  16.0 0.6 slice_convert_fusion.wrem_ref
  16.6 0.6 slice.32.wmain_ref
  17.2 0.6 convert_element_type.21.cls_ref
  17.8 0.0 copy-done
  17.8 0.6 pad.4.wo_ref
  18.5 0.9 copy.18
  19.5 3.0 %concatenate.15.table_hbm = bf16[1152,208]{1,0:T(8,128)(2,1)} concatenate(bf16[1152,192]{1,0:T(8,128)(2,1)} %constant.57.clone, bf16[1152,4]{1,0:T(8,128)(2,1)S(1)} %bitcast.12, bf16[1152,4]{1,0:T(8,128)(2,1)S(1)} %bitcast.13, bf16[1152,4]{1,0:T(8,128)(2,1)S(1)} %bitcast.14, bf16[1152,4]{1,0:T(8,128)(2,1)S(1)} %broadcast_in_dim.15), dimensions={1} | concatenate | bytes 958464 | tf_op jit(solution)/shard_map/concatenate | solution.py:391
  22.5 0.0 copy-done.1
  22.5 1.6 %copy.19.mod_hbm = bf16[1152,432]{1,0:T(8,128)(2,1)} copy(bf16[1152,432]{0,1:T(8,128)(2,1)S(1)} %copy-done.1) | data formatting | bytes 1990656 | tf_op args[8]
  24.1 92.8 %shard_map.149 = (f32[1,4,4,128]{3,2,1,0:T(4,128)}, f32[4,1]{1,0:T(4,128)}) custom-call(f32[3]{0:T(128)} %pad_maximum_fusion.1.coef_ref, f32[1,4,4,128]{3,2,1,0:T(4,128)} %lat_ref.1, f32[4,4,128]{2,1,0:T(4,128)} %anchor_ref.1, f32[1,4,4,128]{3,2,1,0:T(4,128)} %noise_ref.1, f32[1,256]{1,0:T(1,128)} %bitcast.15, f32[8,1152]{1,0:T(8,128)} %convert_element_type.21.cls_ref, ...), custom_call_target="tpu_custom_call" | custom-call | flops 6000000000 | bytes 8000000 | tf_op jit(solution)/shard_map/pallas_call | solution.py:397
  116.9 1.3 %reduce = f32[4]{0:T(128)} reduce(f32[4,1]{1,0:T(4,128)} %get-tuple-element.5, f32[]{:T(128)} %constant.68), dimensions={1}, to_apply=%get-tuple-element.5.reduce_sub_computation | reduce | bytes 36 | tf_op jit(solution)/shard_map/pallas_call | solution.py:397
  118.2 1.3 %copy.21 = f32[1,4,4,128]{3,2,1,0:T(4,128)} copy(f32[1,4,4,128]{3,2,1,0:T(4,128)} %get-tuple-element.23) | data formatting | bytes 16384
  (5 shorter events, 0.1 us)
Async XLA Ops:
  0.6 17.2 %copy-start = (bf16[9,1152]{1,0:T(8,128)(2,1)S(1)}, bf16[9,1152]{1,0:T(8,128)(2,1)}, u32[]{:S(2)}) copy-start(bf16[9,1152]{1,0:T(8,128)(2,1)} %param.24) | copy-start | bytes 62212
  0.6 21.8 %copy-start.1 = (bf16[1152,432]{0,1:T(8,128)(2,1)S(1)}, bf16[1152,432]{0,1:T(8,128)(2,1)}, u32[]{:S(2)}) copy-start(bf16[1152,432]{0,1:T(8,128)(2,1)} %param.22) | copy-start | bytes 2985988

commit v2 on v1

v2 whole, which is shorter than its diff:
```python
import math

import jax
import jax.numpy as jnp
import ml_dtypes
import numpy as np
from jax import lax
from jax.experimental import pallas as pl
from jax.experimental.pallas import tpu as pltpu
from jax.sharding import PartitionSpec as P

MESH = pl.DeviceIdType.MESH
D = 1152
HEAD = 72
HEADS = 8
CHAN = 4
CLASSES = 1000
FREQ = 256
SIDE = 32
TOKENS = 1024
IMAGES = 4
NX, NZ, NT = 4, 16, 8
SLOTS = NX * NZ
HP = 80
CHUNK = 9
PIECE = 48
HALF = 512
F32 = jnp.float32
BF16 = jnp.bfloat16


def split3(values):
    high = values.astype(BF16).astype(F32)
    rest = values - high
    mid = rest.astype(BF16).astype(F32)
    return high, mid, rest - mid


def split2(values):
    high = values.astype(BF16)
    return high, (values - high.astype(F32)).astype(BF16)


def position_constants():
    quarter = D // 4
    angular = np.exp(np.float32(-math.log(10000.0)) * np.arange(quarter, dtype=np.float32) / np.float32(quarter)).astype(np.float32)
    angles = (np.arange(SIDE, dtype=np.float32)[:, None] * angular[None, :]).astype(np.float64)
    pair = np.concatenate([np.sin(angles), np.cos(angles)], axis=1)
    table = np.zeros((D, 128))
    table[: D // 2, 0:SIDE] = pair.T
    table[D // 2 :, SIDE : 2 * SIDE] = pair.T
    table = table - table.mean(axis=0, keepdims=True)
    tokens = np.arange(TOKENS)
    spread = (table[:, tokens // SIDE] + table[:, SIDE + tokens % SIDE]) ** 2
    half_freq = FREQ // 2
    freq = np.exp(-math.log(10000.0) * np.arange(half_freq) / half_freq)
    return (
        table.astype(np.float32),
        spread.mean(axis=0)[None, :].astype(np.float32),
        freq[None, :].astype(np.float32),
    )


def signal_level(step_value):
    return 0.005 + 0.99 * jnp.cos(0.4 * math.pi * step_value / 1000.0) ** 2


def coefficients(t_from, t_to):
    level_from = signal_level(t_from)
    level_to = signal_level(t_to)
    keep_coef = jnp.sqrt(level_to / level_from)
    noise_coef = 0.5 * jnp.sqrt((1.0 - level_to) / (1.0 - level_from)) * jnp.sqrt(1.0 - level_from / level_to)
    eps_coef = jnp.sqrt(1.0 - level_to - noise_coef * noise_coef) - keep_coef * jnp.sqrt(1.0 - level_from)
    return (keep_coef, noise_coef, eps_coef)


def kernel(
    steps_ref, labels_ref, lat_ref, anchor_ref, noise_ref, freq_ref, cls_ref, fw_ref, inw_ref, spread_ref,
    wq_ref, wo_ref, time_hbm, mod_hbm, table_hbm,
    upd_ref, err_ref,
    time_w, mod_w, table, tcat, xs, xo, psrc, pr, mod_s, mod_r, mod_t, rb, ab, shifts,
    zw, zr, wf, wx, wt, zo, po, of, wob, emb, own, att_s, att_r,
    dr_r, tx_r, er_r, er_s, invs,
    loc_sem, pr_send, pr_recv, mod_send, mod_recv, zw_send, zw_recv, zr_send, zr_recv,
    wx_send, wx_recv, zo_send, zo_recv, ox_send, ox_recv, sib_send, sib_recv,
    att_send, att_recv, dr_send, dr_recv, tx_send, tx_recv, er_send, er_recv,
):
    slot = lax.axis_index("tm")
    tok = lax.axis_index("tok")
    x = lax.div(slot, NZ)
    z = lax.rem(slot, NZ)
    core = lax.rem(tok, 2)
    sibling = tok + 1 - 2 * core

    def z_peer(k):
        return (x * NZ + lax.rem(z + k, NZ), tok)

    def x_peer(k):
        return (lax.rem(x + k, NX) * NZ + z, tok)

    def t_peer(k):
        return (slot, lax.rem(tok + k, NT))

    def each(count, action, first=1):
        def step(k, carry):
            action(k)
            return carry

        lax.fori_loop(first, count, step, 0)

    def remote(src, dst, send, recv, device):
        return pltpu.make_async_remote_copy(
            src_ref=src, dst_ref=dst, send_sem=send, recv_sem=recv, device_id=device, device_id_type=MESH
        )

    loads = [
        pltpu.make_async_copy(time_hbm, time_w, loc_sem.at[0]),
        pltpu.make_async_copy(mod_hbm, mod_w, loc_sem.at[1]),
        pltpu.make_async_copy(table_hbm, table, loc_sem.at[2]),
    ]
    for load in loads:
        load.start()

    barrier = pltpu.get_barrier_semaphore()

    def greet(device):
        pl.semaphore_signal(barrier, inc=1, device_id=device, device_id_type=MESH)

    each(NZ, lambda k: greet(z_peer(k)))
    each(NX, lambda k: greet(x_peer(k)))
    each(NT, lambda k: greet(t_peer(k)))
    before = lax.rem(slot + SLOTS - 1, SLOTS)
    after = lax.rem(slot + 1, SLOTS)
    each(NT, lambda k: greet((before, k)), first=0)
    psrc[...] = jnp.where(slot == SLOTS - 1, anchor_ref[...], lat_ref[0])
    for t in range(NT):

        @pl.when(tok == t)
        def _():
            wide = wq_ref[...].astype(F32)
            cols = [wide[:, HEAD * (HEADS * i + t) : HEAD * (HEADS * i + t + 1)] for i in range(3)]
            packed = jnp.concatenate(cols + [jnp.zeros((18, 40), F32)], axis=1)
            zw[z] = packed[0:16].astype(BF16)
            zr[z] = packed[16:18]

    grid = lax.broadcasted_iota(jnp.int32, (SIDE, TOKENS), 1)
    line = lax.broadcasted_iota(jnp.int32, (SIDE, TOKENS), 0)
    chosen = [jnp.where(line == (grid >> 5), 1.0, 0.0), jnp.where(line == (grid & 31), 1.0, 0.0)]
    chosen = jnp.concatenate(chosen + [jnp.zeros((64, TOKENS), F32)], axis=0).astype(BF16)
    xs[0:128] = chosen
    xs[128:256] = chosen
    po[...] = jnp.zeros((PIECE, 128), F32)
    for c in range(2):

        @pl.when(core == c)
        def _():
            wide = wo_ref[...].astype(F32)
            for i in range(5 - c):
                k = 5 * c + i
                po[CHUNK * i : CHUNK * i + CHUNK] = wide[:, 128 * k : 128 * k + 128]

    zo[z] = po[...].astype(BF16)
    pl.semaphore_wait(barrier, NZ - 1 + NX - 1 + NT - 1 + NT)

    def prior_copy(k):
        return remote(psrc, pr.at[tok], pr_send.at[k], pr_recv.at[tok], (after, k))

    def prior_arrival(k):
        return remote(psrc, pr.at[k], pr_send.at[k], pr_recv.at[k], (after, k))

    def zw_copy(k):
        return remote(zw.at[z], zw.at[z], zw_send.at[k], zw_recv.at[k], z_peer(k))

    def zr_copy(k):
        return remote(zr.at[z], zr.at[z], zr_send.at[k], zr_recv.at[k], z_peer(k))

    def zo_copy(k):
        return remote(zo.at[z], zo.at[z], zo_send.at[k], zo_recv.at[k], z_peer(k))

    def wx_copy(k):
        return remote(wx.at[x], wx.at[x], wx_send.at[k], wx_recv.at[k], x_peer(k))

    def ox_copy(k):
        return remote(wob.at[core, x], wob.at[core, x], ox_send.at[k], ox_recv.at[k], x_peer(k))

    def mod_copy(k):
        return remote(mod_s, mod_r.at[tok], mod_send.at[k], mod_recv.at[k], t_peer(k))

    def att_copy(b, k):
        there = lax.rem(tok + k, NT)
        return remote(att_s.at[b, there], att_r.at[b, tok], att_send.at[b, k], att_recv.at[b, k], t_peer(k))

    each(NT, lambda k: prior_copy(k).start(), first=0)

    def start_w(k):
        zw_copy(k).start()
        zr_copy(k).start()

    each(NZ, start_w)

    t_from = jnp.full((1, 128), steps_ref[0, 0].astype(F32))
    t_to = jnp.full((1, 128), steps_ref[0, 1].astype(F32))
    phases = t_from * freq_ref[...]
    features = jnp.concatenate([jnp.cos(phases), jnp.sin(phases)], axis=1)
    high, mid, low = split3(features)
    feats = jnp.concatenate([high, mid, low, jnp.zeros((5, FREQ), F32)], axis=0).astype(BF16)
    row8 = lax.broadcasted_iota(jnp.int32, (8, CLASSES), 0)
    col8 = lax.broadcasted_iota(jnp.int32, (8, CLASSES), 1)
    hot = jnp.zeros((8, CLASSES), F32)
    for b in range(IMAGES):
        hot = hot + jnp.where((row8 == b) & (col8 == labels_ref[b]), 1.0, 0.0)
    classes = jnp.dot(hot.astype(BF16), cls_ref[...], preferred_element_type=F32)
    loads[0].wait()
    parts = jnp.dot(feats, time_w[...], preferred_element_type=F32)
    value = parts[0:1] + parts[1:2] + parts[2:3] + classes
    condition = (value / (1.0 + jnp.exp(-value))).astype(BF16)
    loads[1].wait()
    mod_s[:, 432:512] = jnp.zeros((8, 80), F32)
    mod_s[:, 0:432] = lax.dot_general(
        condition, mod_w[...], (((1,), (1,)), ((), ())), preferred_element_type=F32
    )
    mod_r[tok] = mod_s[...]
    each(NT, lambda k: mod_copy(k).start())

    loads[2].wait()
    inw = inw_ref[...].astype(F32)
    inw = inw - jnp.mean(inw, axis=1, keepdims=True)
    pad = jnp.concatenate([jnp.zeros((64, D), F32), inw, inw, jnp.zeros((56, D), F32)], axis=0)
    centred = table[...] + jnp.transpose(pad)
    table[...] = centred
    high, low = split2(centred)
    tcat[:, 0:128] = high
    tcat[:, 128:256] = low
    inner = jnp.dot(
        jnp.concatenate([inw, inw], axis=0), centred, preferred_element_type=F32, precision=lax.Precision.HIGHEST
    )
    lane = lax.broadcasted_iota(jnp.int32, (8, 128), 1)
    cross = jnp.where(lane < 64, inner, 0.0)
    crosses = jnp.concatenate(list(split3(cross)) + [jnp.zeros((8, 128), F32)], axis=0).astype(BF16)
    crosses = jnp.dot(crosses, xs[0:128], preferred_element_type=F32)
    crosses = (crosses[0:8] + crosses[8:16] + crosses[16:24])[0:CHAN]

    each(NT, lambda k: mod_copy(k).wait())
    for source in range(NT):
        mod_t[source * 432 : source * 432 + 432] = jnp.transpose(mod_r[source])[0:432]
    rows = 128

    def gains(r, carry):
        here = pl.ds(pl.multiple_of(r * rows, rows), rows)
        shift = mod_t[here]
        gain = 1.0 + mod_t[pl.ds(pl.multiple_of(D + r * rows, rows), rows)]
        lanes = lax.broadcasted_iota(jnp.int32, (rows, 128), 1)
        base = table[here]
        for b in range(IMAGES):
            value = jnp.where(lanes == 72, shift[:, b : b + 1], gain[:, b : b + 1] * base)
            high, low = split2(value)
            rb[here, 256 * b : 256 * b + 128] = high
            rb[here, 256 * b + 128 : 256 * b + 256] = low
        return carry

    lax.fori_loop(0, D // rows, gains, 0)
    each(NT, lambda k: prior_arrival(k).wait(), first=0)

    def place(b):
        line = jnp.concatenate([pr[t, b] for t in range(NT)], axis=1)
        high = line.astype(BF16).astype(F32)
        low = line - high
        nought = jnp.zeros((CHAN, TOKENS), F32)
        xs[64:80] = jnp.concatenate([high, low, nought, nought], axis=0).astype(BF16)
        xs[192:208] = jnp.concatenate([high, nought, nought, nought], axis=0).astype(BF16)
        return line

    for b in range(IMAGES):
        line = place(b)
        squares = 2.0 * crosses
        for c in range(CHAN):
            squares = squares + inner[0:CHAN, 64 + c : 65 + c] * line[c : c + 1]
        variance = spread_ref[...] + jnp.sum(line * squares, axis=0, keepdims=True) * (1.0 / D)
        invs[b] = lax.rsqrt(jnp.maximum(variance, 0.0) + 1e-06)
        xo[:, b * 128 : b * 128 + 128] = xs[:, pl.ds(pl.multiple_of(tok * 128, 128), 128)]

    def arrive_w(k):
        zw_copy(k).wait()
        zr_copy(k).wait()

    each(NZ, arrive_w)
    each(NZ, lambda k: zo_copy(k).start())
    for i in range(NZ):
        wf[18 * i : 18 * i + 16] = zw[i].astype(F32)
        wf[18 * i + 16 : 18 * i + 18] = zr[i]
    wx[x] = wf[...].astype(BF16)
    each(NX, lambda k: wx_copy(k).start())
    own[...] = jnp.dot(tcat[...], xo[...], preferred_element_type=F32)
    each(NX, lambda k: wx_copy(k).wait())
    wt[...] = jnp.transpose(wx[...].reshape(D, 256))
    folded = jnp.dot(wt[...], rb[...], preferred_element_type=F32)
    for b in range(IMAGES):
        both = folded[:, 256 * b : 256 * b + 128] + folded[:, 256 * b + 128 : 256 * b + 256]
        high, low = split2(both)
        ab[b, :, 0:128] = high
        ab[b, :, 128:256] = low
        shifts[b] = jnp.broadcast_to(both[:, 72:73], (256, 128))

    factor = math.log2(math.e) / math.sqrt(HEAD)
    block = 256

    def attend(b, carry):
        place(b)
        shift = jnp.concatenate([shifts[b]] * NT, axis=1)
        qkv = jnp.dot(ab[b], xs[...], preferred_element_type=F32) * invs[b] + shift
        queries = jnp.concatenate([qkv[0:HEAD], jnp.zeros((128 - HEAD, TOKENS), F32)], axis=0).astype(BF16)
        keys = jnp.transpose(qkv[HEAD : HEAD + 128]).astype(BF16)
        values = jnp.concatenate([qkv[2 * HEAD : 3 * HEAD], jnp.ones((8, TOKENS), F32)], axis=0).astype(BF16)
        for i in range(TOKENS // block):
            scores = jnp.dot(keys, queries[:, i * block : (i + 1) * block], preferred_element_type=F32)
            weights = jnp.exp2(scores * factor).astype(BF16)
            summed = jnp.dot(values, weights, preferred_element_type=F32)
            out = (summed / summed[HEAD : HEAD + 1]).astype(BF16)
            for t in range(2):
                att_s[b, 2 * i + t] = out[:, t * 128 : t * 128 + 128]
        att_r[b, tok] = att_s[b, tok]
        each(NT, lambda k: att_copy(b, k).start())
        return carry

    lax.fori_loop(0, 1, attend, 0)

    each(NZ, lambda k: zo_copy(k).wait())
    for i in range(NZ):
        base = 9 * i + (HP - HEAD) * (i // 8)
        piece = zo[i].astype(F32)
        for k in range(5):
            of[base : base + CHUNK, 128 * k : 128 * k + 128] = piece[CHUNK * k : CHUNK * k + CHUNK]
    for h in range(2):
        of[h * HP + HEAD : (h + 1) * HP] = jnp.zeros((HP - HEAD, 640), F32)
    wob[core, x] = of[...].astype(BF16)
    each(NX, lambda k: ox_copy(k).start())
    lax.fori_loop(1, 4, attend, 0)
    each(NX, lambda k: ox_copy(k).wait())
    share = remote(wob.at[core], wob.at[core], sib_send, sib_recv, (slot, sibling))
    share.start()
    other = remote(wob.at[1 - core], wob.at[1 - core], sib_send, sib_recv, (slot, sibling))
    each(NT, lambda k: [att_copy(b, k).wait() for b in range(IMAGES)])
    share.wait_send()
    other.wait_recv()

    attended = jnp.concatenate([att_r[b].reshape(HEADS * HP, 128) for b in range(IMAGES)], axis=1)
    contract = (((0,), (0,)), ((), ()))
    emb[0:640] = lax.dot_general(wob[0].reshape(HEADS * HP, 640), attended, contract, preferred_element_type=F32)
    emb[640:D] = lax.dot_general(wob[1].reshape(HEADS * HP, 640)[:, 0:512], attended, contract, preferred_element_type=F32)

    def hidden(r, total):
        here = pl.ds(pl.multiple_of(r * rows, rows), rows)
        gates = mod_t[pl.ds(pl.multiple_of(2 * D + r * rows, rows), rows)]
        sums = []
        for b in range(IMAGES):
            cut = slice(b * 128, b * 128 + 128)
            value = own[here, cut] + gates[:, b : b + 1] * emb[here, cut]
            emb[here, cut] = value
            sums.append(jnp.sum(value.reshape(rows // 8, 8, 128), axis=0))
        return total + jnp.concatenate(sums, axis=1)

    total = lax.fori_loop(0, D // rows, hidden, jnp.zeros((8, HALF), F32))
    mean = jnp.sum(total, axis=0, keepdims=True) * (1.0 / D)

    def square(r, total):
        chunk = emb[pl.ds(pl.multiple_of(r * rows, rows), rows)] - mean
        return total + jnp.sum((chunk * chunk).reshape(rows // 8, 8, HALF), axis=0)

    total = lax.fori_loop(0, D // rows, square, jnp.zeros((8, HALF), F32))
    inverse = lax.rsqrt(jnp.sum(total, axis=0, keepdims=True) * (1.0 / D) + 1e-06)
    final = ((emb[...] - mean) * inverse).astype(BF16)
    predicted = jnp.dot(fw_ref[...], final, preferred_element_type=F32)

    keep, noise, eps = coefficients(t_from, t_to)
    for b in range(IMAGES):
        dr_r[z, b] = (keep - 1.0) * pr[tok, b] + eps * predicted[0:CHAN, b * 128 : b * 128 + 128] + noise * noise_ref[0, b]

    def dr_copy(k):
        return remote(dr_r.at[z], dr_r.at[z], dr_send.at[k], dr_recv.at[k], z_peer(k))

    def tx_copy(k):
        return remote(tx_r.at[x], tx_r.at[x], tx_send.at[k], tx_recv.at[k], x_peer(k))

    each(NZ, lambda k: dr_copy(k).start())
    each(NZ, lambda k: dr_copy(k).wait())
    nothing = jnp.zeros((IMAGES, CHAN, 128), F32)
    whole, reached = nothing, nothing
    for i in range(NZ):
        term = dr_r[i]
        whole = whole + term
        reached = reached + jnp.where(i <= z, term, nothing)
    tx_r[x] = whole
    each(NX, lambda k: tx_copy(k).start())
    each(NX, lambda k: tx_copy(k).wait())
    earlier = nothing
    for i in range(NX):
        earlier = earlier + jnp.where(i < x, tx_r[i], nothing)
    updated = anchor_ref[...] + (earlier + reached)
    upd_ref[0] = updated
    change = updated - lat_ref[0]
    er_s[...] = jnp.sum(change * change, axis=1)
    er_r[tok] = er_s[...]

    def er_copy(k):
        return remote(er_s, er_r.at[tok], er_send.at[k], er_recv.at[k], t_peer(k))

    each(NT, lambda k: er_copy(k).start())
    each(NT, lambda k: er_copy(k).wait())
    summed = jnp.sum(jnp.sum(er_r[...], axis=0), axis=1, keepdims=True) * (1.0 / (CHAN * TOKENS))
    spot = lax.broadcasted_iota(jnp.int32, (IMAGES, 128), 0) == lax.broadcasted_iota(jnp.int32, (IMAGES, 128), 1)
    err_ref[...] = jnp.sum(jnp.where(spot, summed, 0.0), axis=0, keepdims=True)[:, 0:IMAGES]


def body(
    anchor, latents, noise_draws, slot_steps, class_labels, in_weight, time_weight, class_table,
    mod_weight, qkv_weight, out_weight, final_weight,
):
    table, spread, freq = (jnp.asarray(value) for value in position_constants())
    vmem = pl.BlockSpec(memory_space=pltpu.VMEM)
    anywhere = pl.BlockSpec(memory_space=pl.ANY)
    dma = pltpu.SemaphoreType.DMA
    updated, errors = pl.pallas_call(
        kernel,
        out_shape=(
            jax.ShapeDtypeStruct((1, IMAGES, CHAN, 128), F32),
            jax.ShapeDtypeStruct((1, IMAGES), F32),
        ),
        in_specs=[pl.BlockSpec(memory_space=pltpu.SMEM)] * 2 + [vmem] * 10 + [anywhere] * 3,
        out_specs=(vmem, vmem),
        scratch_shapes=[
            pltpu.VMEM((FREQ, D), BF16),
            pltpu.VMEM((432, D), BF16),
            pltpu.VMEM((D, 128), F32),
            pltpu.VMEM((D, 256), BF16),
            pltpu.VMEM((256, TOKENS), BF16),
            pltpu.VMEM((256, HALF), BF16),
            pltpu.VMEM((IMAGES, CHAN, 128), F32),
            pltpu.VMEM((NT, IMAGES, CHAN, 128), F32),
            pltpu.VMEM((8, 512), F32),
            pltpu.VMEM((NT, 8, 512), F32),
            pltpu.VMEM((3 * D, 8), F32),
            pltpu.VMEM((D, 256 * IMAGES), BF16),
            pltpu.VMEM((IMAGES, 256, 256), BF16),
            pltpu.VMEM((IMAGES, 256, 128), F32),
            pltpu.VMEM((NZ, 16, 256), BF16),
            pltpu.VMEM((NZ, 2, 256), F32),
            pltpu.VMEM((18 * NZ, 256), F32),
            pltpu.VMEM((NX, 18 * NZ, 256), BF16),
            pltpu.VMEM((256, D), BF16),
            pltpu.VMEM((NZ, PIECE, 128), BF16),
            pltpu.VMEM((PIECE, 128), F32),
            pltpu.VMEM((2 * HP, 640), F32),
            pltpu.VMEM((2, NX, 2 * HP, 640), BF16),
            pltpu.VMEM((D, HALF), F32),
            pltpu.VMEM((D, HALF), F32),
            pltpu.VMEM((IMAGES, NT, HP, 128), BF16),
            pltpu.VMEM((IMAGES, NT, HP, 128), BF16),
            pltpu.VMEM((NZ, IMAGES, CHAN, 128), F32),
            pltpu.VMEM((NX, IMAGES, CHAN, 128), F32),
            pltpu.VMEM((NT, IMAGES, 128), F32),
            pltpu.VMEM((IMAGES, 128), F32),
            pltpu.VMEM((IMAGES, 1, TOKENS), F32),
            dma((3,)),
            dma((NT,)), dma((NT,)),
            dma((NT,)), dma((NT,)),
            dma((NZ,)), dma((NZ,)),
            dma((NZ,)), dma((NZ,)),
            dma((NX,)), dma((NX,)),
            dma((NZ,)), dma((NZ,)),
            dma((NX,)), dma((NX,)),
            dma, dma,
            dma((IMAGES, NT)), dma((IMAGES, NT)),
            dma((NZ,)), dma((NZ,)),
            dma((NX,)), dma((NX,)),
            dma((NT,)), dma((NT,)),
        ],
        compiler_params=pltpu.CompilerParams(
            collective_id=0, has_side_effects=True, vmem_limit_bytes=56 * 1024 * 1024
        ),
        cost_estimate=pl.CostEstimate(flops=6_000_000_000, bytes_accessed=8_000_000, transcendentals=4_200_000),
    )(
        slot_steps, class_labels, latents, anchor, noise_draws, freq, class_table, final_weight, in_weight, spread,
        qkv_weight, out_weight, time_weight, mod_weight.T, table,
    )
    return updated, errors


def solution(mesh):
    in_specs = (
        P(None, None, "tok"),
        P("tm", None, None, "tok"),
        P("tm", None, None, "tok"),
        P("tm", None),
        P(),
        P(),
        P(),
        P(),
        P(None, "tok"),
        P("tm", None),
        P("tm", None),
        P(),
    )
    out_specs = (P("tm", None, None, "tok"), P("tm", None))
    return jax.shard_map(body, mesh=mesh, in_specs=in_specs, out_specs=out_specs, check_vma=False)
```

time: 120 us -> 81 us (0.68)
  Pallas kernels: 92.8 us -> 77.7 us
  local copies, waits for them, and re-layouts: 12.7 us -> 2.43 us
  between operations: 10.1 us -> 0.64 us
  other arithmetic: 3.85 us -> 0 us
    pallas_call x1, Pallas kernels: 92.8 us -> 77.7 us  [body(): pl.pallas_call(kernel, out_shape=(jax.ShapeDtypeStruct((1, IMAGES, CHAN,...]
    slice x3 -> x0, local copies, waits for them, and re-layouts: 3.39 us -> none  [the longest x1 1.47 us: body(): class_labels[b]]
    concatenate x3 -> x0, local copies, waits for them, and re-layouts: 3.15 us -> none  [the longest x1 3.02 us: body(): jnp.concatenate([jnp.asarray(table), turned, turned, turned, jnp.zeros((D...]
    dynamic_slice x3 -> x0, local copies, waits for them, and re-layouts: 1.64 us -> none  [the longest x1 0.83 us: body(): lax.dynamic_slice(qkv_weight, (0, HEAD * (HEADS * i + tok)), (18, HEAD))]
    unnamed x7 -> x2, local copies, waits for them, and re-layouts: 3.87 us -> 2.43 us
    pallas_call x1 -> x0, other arithmetic: 1.29 us -> none  [body(): pl.pallas_call(kernel, out_shape=(jax.ShapeDtypeStruct((1, IMAGES, CHAN,...]
    convert_element_type x2 -> x0, other arithmetic: 1.21 us -> none  [the longest x1 0.61 us: body(): classes = jnp.concatenate([lax.dynamic_slice(class_table, (class_labels[b...]
where the time goes in v2:
time: 81 us; the launch traced here: 80.8 us
  Pallas kernels  77.7 us (96%)
  local copies, waits for them, and re-layouts  2.43 us (3%)
    pallas_call x1, Pallas kernels, body(): pl.pallas_call(kernel, out_shape=(jax.ShapeDtypeStruct((1, IMAGES, CHAN,...  77.7 us
    unnamed x2, local copies, waits for them, and re-layouts  2.43 us

profile of v2, /device:TPU:1, one launch (start us, length us, event | category | flops | bytes accessed | tf_op | source)
XLA Modules:
  0.0 80.8 jit_solution(8012417959923026893)
XLA Ops:
  0.6 77.7 %shard_map.158 = (f32[1,4,4,128]{3,2,1,0:T(4,128)}, f32[1,4]{1,0:T(1,128)}) custom-call(s32[1,2]{1,0:T(1,128)} %steps_ref.1, s32[4]{0:T(128)} %labels_ref.1, f32[1,4,4,128]{3,2,1,0:T(4,128)} %lat_ref.1, f32[4,4,128]{2,1,0:T(4,128)} %anchor_ref.1, f32[1,4,4,128]{3,2,1,0:T(4,128)} %noise_ref.1, f32[1,128]{1,0:T(1,128)} %constant.8.clone.freq_ref, ...), custom_call_target="tpu_custom_call" | custom-call | flops 6000000000 | bytes 8000000 | tf_op jit(solution)/shard_map/pallas_call | solution.py:422
  78.3 1.3 %copy.19 = f32[1,4,4,128]{3,2,1,0:T(4,128)} copy(f32[1,4,4,128]{3,2,1,0:T(4,128)} %get-tuple-element.4) | data formatting | bytes 16384
  79.6 1.1 %copy.20 = f32[1,4]{1,0:T(1,128)} copy(f32[1,4]{1,0:T(1,128)} %get-tuple-element.5) | data formatting | bytes 32

commit v3 on v2

--- a/solution.py
+++ b/solution.py
@@ -77,10 +77,10 @@
 def kernel(
     steps_ref, labels_ref, lat_ref, anchor_ref, noise_ref, freq_ref, cls_ref, fw_ref, inw_ref, spread_ref,
     wq_ref, wo_ref, time_hbm, mod_hbm, table_hbm,
-    upd_ref, err_ref,
+    out_ref,
     time_w, mod_w, table, tcat, xs, xo, psrc, pr, mod_s, mod_r, mod_t, rb, ab, shifts,
     zw, zr, wf, wx, wt, zo, po, of, wob, emb, own, att_s, att_r,
-    dr_r, tx_r, er_r, er_s, invs,
+    dr_r, sc_s, sc_r, tx_r, er_r, er_s, invs,
     loc_sem, pr_send, pr_recv, mod_send, mod_recv, zw_send, zw_recv, zr_send, zr_recv,
     wx_send, wx_recv, zo_send, zo_recv, ox_send, ox_recv, sib_send, sib_recv,
     att_send, att_recv, dr_send, dr_recv, tx_send, tx_recv, er_send, er_recv,
@@ -92,6 +92,11 @@
     core = lax.rem(tok, 2)
     sibling = tok + 1 - 2 * core
 
+    kind, turn = lax.rem(z, 4), lax.div(z, 4)
+    place_z = 4 * kind + turn
+    family = pl.ds(pl.multiple_of(4 * kind, 4), 4)
+    near = (0, 1, NZ - 1, 2)
+
     def z_peer(k):
         return (x * NZ + lax.rem(z + k, NZ), tok)
 
@@ -102,11 +107,8 @@
         return (slot, lax.rem(tok + k, NT))
 
     def each(count, action, first=1):
-        def step(k, carry):
+        for k in range(first, count):
             action(k)
-            return carry
-
-        lax.fori_loop(first, count, step, 0)
 
     def remote(src, dst, send, recv, device):
         return pltpu.make_async_remote_copy(
@@ -126,7 +128,8 @@
     def greet(device):
         pl.semaphore_signal(barrier, inc=1, device_id=device, device_id_type=MESH)
 
-    each(NZ, lambda k: greet(z_peer(k)))
+    each(4, lambda k: greet(z_peer(4 * k)))
+    each(4, lambda k: greet(z_peer(NZ - near[k])))
     each(NX, lambda k: greet(x_peer(k)))
     each(NT, lambda k: greet(t_peer(k)))
     before = lax.rem(slot + SLOTS - 1, SLOTS)
@@ -140,8 +143,8 @@
             wide = wq_ref[...].astype(F32)
             cols = [wide[:, HEAD * (HEADS * i + t) : HEAD * (HEADS * i + t + 1)] for i in range(3)]
             packed = jnp.concatenate(cols + [jnp.zeros((18, 40), F32)], axis=1)
-            zw[z] = packed[0:16].astype(BF16)
-            zr[z] = packed[16:18]
+            zw[place_z] = packed[0:16].astype(BF16)
+            zr[place_z] = packed[16:18]
 
     grid = lax.broadcasted_iota(jnp.int32, (SIDE, TOKENS), 1)
     line = lax.broadcasted_iota(jnp.int32, (SIDE, TOKENS), 0)
@@ -159,8 +162,8 @@
                 k = 5 * c + i
                 po[CHUNK * i : CHUNK * i + CHUNK] = wide[:, 128 * k : 128 * k + 128]
 
-    zo[z] = po[...].astype(BF16)
-    pl.semaphore_wait(barrier, NZ - 1 + NX - 1 + NT - 1 + NT)
+    zo[place_z] = po[...].astype(BF16)
+    pl.semaphore_wait(barrier, 3 + 3 + NX - 1 + NT - 1 + NT)
 
     def prior_copy(k):
         return remote(psrc, pr.at[tok], pr_send.at[k], pr_recv.at[tok], (after, k))
@@ -168,14 +171,27 @@
     def prior_arrival(k):
         return remote(psrc, pr.at[k], pr_send.at[k], pr_recv.at[k], (after, k))
 
-    def zw_copy(k):
-        return remote(zw.at[z], zw.at[z], zw_send.at[k], zw_recv.at[k], z_peer(k))
-
-    def zr_copy(k):
-        return remote(zr.at[z], zr.at[z], zr_send.at[k], zr_recv.at[k], z_peer(k))
-
-    def zo_copy(k):
-        return remote(zo.at[z], zo.at[z], zo_send.at[k], zo_recv.at[k], z_peer(k))
+    def far_copies(pairs, k):
+        return [
+            remote(ref.at[place_z], ref.at[place_z], send.at[k], recv.at[k], z_peer(4 * k)) for ref, send, recv in pairs
+        ]
+
+    def near_copies(pairs, k):
+        return [
+            remote(ref.at[family], ref.at[family], send.at[3 + k], recv.at[3 + k], z_peer(near[k]))
+            for ref, send, recv in pairs
+        ]
+
+    w_pairs = [(zw, zw_send, zw_recv), (zr, zr_send, zr_recv)]
+    o_pairs = [(zo, zo_send, zo_recv)]
+
+    def start(copies):
+        for copy in copies:
+            copy.start()
+
+    def finish(copies):
+        for copy in copies:
+            copy.wait()
 
     def wx_copy(k):
         return remote(wx.at[x], wx.at[x], wx_send.at[k], wx_recv.at[k], x_peer(k))
@@ -192,11 +208,7 @@
 
     each(NT, lambda k: prior_copy(k).start(), first=0)
 
-    def start_w(k):
-        zw_copy(k).start()
-        zr_copy(k).start()
-
-    each(NZ, start_w)
+    each(4, lambda k: start(far_copies(w_pairs, k)))
 
     t_from = jnp.full((1, 128), steps_ref[0, 0].astype(F32))
     t_to = jnp.full((1, 128), steps_ref[0, 1].astype(F32))
@@ -221,6 +233,8 @@
     )
     mod_r[tok] = mod_s[...]
     each(NT, lambda k: mod_copy(k).start())
+    each(4, lambda k: finish(far_copies(w_pairs, k)))
+    each(4, lambda k: start(near_copies(w_pairs, k)))
 
     loads[2].wait()
     inw = inw_ref[...].astype(F32)
@@ -243,6 +257,15 @@
     each(NT, lambda k: mod_copy(k).wait())
     for source in range(NT):
         mod_t[source * 432 : source * 432 + 432] = jnp.transpose(mod_r[source])[0:432]
+
+    each(4, lambda k: finish(near_copies(w_pairs, k)))
+    each(4, lambda k: start(far_copies(o_pairs, k)))
+    for i in range(NZ):
+        member = 4 * (i % 4) + i // 4
+        wf[18 * i : 18 * i + 16] = zw[member].astype(F32)
+        wf[18 * i + 16 : 18 * i + 18] = zr[member]
+    wx[x] = wf[...].astype(BF16)
+    each(NX, lambda k: wx_copy(k).start())
     rows = 128
 
     def gains(r, carry):
@@ -259,6 +282,8 @@
         return carry
 
     lax.fori_loop(0, D // rows, gains, 0)
+    each(4, lambda k: finish(far_copies(o_pairs, k)))
+    each(4, lambda k: start(near_copies(o_pairs, k)))
     each(NT, lambda k: prior_arrival(k).wait(), first=0)
 
     def place(b):
@@ -279,19 +304,18 @@
         invs[b] = lax.rsqrt(jnp.maximum(variance, 0.0) + 1e-06)
         xo[:, b * 128 : b * 128 + 128] = xs[:, pl.ds(pl.multiple_of(tok * 128, 128), 128)]
 
-    def arrive_w(k):
-        zw_copy(k).wait()
-        zr_copy(k).wait()
-
-    each(NZ, arrive_w)
-    each(NZ, lambda k: zo_copy(k).start())
+    own[...] = jnp.dot(tcat[...], xo[...], preferred_element_type=F32)
+    each(4, lambda k: finish(near_copies(o_pairs, k)))
     for i in range(NZ):
-        wf[18 * i : 18 * i + 16] = zw[i].astype(F32)
-        wf[18 * i + 16 : 18 * i + 18] = zr[i]
-    wx[x] = wf[...].astype(BF16)
-    each(NX, lambda k: wx_copy(k).start())
-    own[...] = jnp.dot(tcat[...], xo[...], preferred_element_type=F32)
+        base = 9 * i + (HP - HEAD) * (i // 8)
+        piece = zo[4 * (i % 4) + i // 4].astype(F32)
+        for k in range(5):
+            of[base : base + CHUNK, 128 * k : 128 * k + 128] = piece[CHUNK * k : CHUNK * k + CHUNK]
+    for h in range(2):
+        of[h * HP + HEAD : (h + 1) * HP] = jnp.zeros((HP - HEAD, 640), F32)
+    wob[core, x] = of[...].astype(BF16)
     each(NX, lambda k: wx_copy(k).wait())
+    each(NX, lambda k: ox_copy(k).start())
     wt[...] = jnp.transpose(wx[...].reshape(D, 256))
     folded = jnp.dot(wt[...], rb[...], preferred_element_type=F32)
     for b in range(IMAGES):
@@ -315,30 +339,19 @@
             scores = jnp.dot(keys, queries[:, i * block : (i + 1) * block], preferred_element_type=F32)
             weights = jnp.exp2(scores * factor).astype(BF16)
             summed = jnp.dot(values, weights, preferred_element_type=F32)
-            out = (summed / summed[HEAD : HEAD + 1]).astype(BF16)
+            out = (summed * (1.0 / summed[HEAD : HEAD + 1])).astype(BF16)
             for t in range(2):
                 att_s[b, 2 * i + t] = out[:, t * 128 : t * 128 + 128]
         att_r[b, tok] = att_s[b, tok]
         each(NT, lambda k: att_copy(b, k).start())
         return carry
 
-    lax.fori_loop(0, 1, attend, 0)
-
-    each(NZ, lambda k: zo_copy(k).wait())
-    for i in range(NZ):
-        base = 9 * i + (HP - HEAD) * (i // 8)
-        piece = zo[i].astype(F32)
-        for k in range(5):
-            of[base : base + CHUNK, 128 * k : 128 * k + 128] = piece[CHUNK * k : CHUNK * k + CHUNK]
-    for h in range(2):
-        of[h * HP + HEAD : (h + 1) * HP] = jnp.zeros((HP - HEAD, 640), F32)
-    wob[core, x] = of[...].astype(BF16)
-    each(NX, lambda k: ox_copy(k).start())
-    lax.fori_loop(1, 4, attend, 0)
+    lax.fori_loop(0, 3, attend, 0)
     each(NX, lambda k: ox_copy(k).wait())
     share = remote(wob.at[core], wob.at[core], sib_send, sib_recv, (slot, sibling))
     share.start()
     other = remote(wob.at[1 - core], wob.at[1 - core], sib_send, sib_recv, (slot, sibling))
+    lax.fori_loop(3, 4, attend, 0)
     each(NT, lambda k: [att_copy(b, k).wait() for b in range(IMAGES)])
     share.wait_send()
     other.wait_recv()
@@ -373,22 +386,39 @@
 
     keep, noise, eps = coefficients(t_from, t_to)
     for b in range(IMAGES):
-        dr_r[z, b] = (keep - 1.0) * pr[tok, b] + eps * predicted[0:CHAN, b * 128 : b * 128 + 128] + noise * noise_ref[0, b]
+        dr_r[turn, b] = (keep - 1.0) * pr[tok, b] + eps * predicted[0:CHAN, b * 128 : b * 128 + 128] + noise * noise_ref[0, b]
 
     def dr_copy(k):
-        return remote(dr_r.at[z], dr_r.at[z], dr_send.at[k], dr_recv.at[k], z_peer(k))
+        return remote(dr_r.at[turn], dr_r.at[turn], dr_send.at[k], dr_recv.at[k], z_peer(4 * k))
+
+    def sc_copy(k):
+        return remote(sc_s.at[k], sc_r.at[k], dr_send.at[3 + k], dr_recv.at[3 + k], z_peer(near[k]))
 
     def tx_copy(k):
         return remote(tx_r.at[x], tx_r.at[x], tx_send.at[k], tx_recv.at[k], x_peer(k))
 
-    each(NZ, lambda k: dr_copy(k).start())
-    each(NZ, lambda k: dr_copy(k).wait())
+    each(4, lambda k: dr_copy(k).start())
+    each(4, lambda k: dr_copy(k).wait())
     nothing = jnp.zeros((IMAGES, CHAN, 128), F32)
-    whole, reached = nothing, nothing
-    for i in range(NZ):
-        term = dr_r[i]
-        whole = whole + term
-        reached = reached + jnp.where(i <= z, term, nothing)
+
+    def upto(last):
+        total = nothing
+        for i in range(4):
+            total = total + jnp.where(i <= last, dr_r[i], nothing)
+        return total
+
+    whole = upto(3)
+    for k in range(1, 4):
+        there = lax.rem(z + near[k], NZ)
+        sc_s[k, 0] = upto(lax.div(there, 4) - jnp.where(kind > lax.rem(there, 4), 1, 0))
+        sc_s[k, 1] = whole
+    each(4, lambda k: sc_copy(k).start())
+    reached = upto(turn)
+    for k in range(1, 4):
+        sc_copy(k).wait()
+    for k in range(1, 4):
+        reached = reached + sc_r[k, 0]
+        whole = whole + sc_r[k, 1]
     tx_r[x] = whole
     each(NX, lambda k: tx_copy(k).start())
     each(NX, lambda k: tx_copy(k).wait())
@@ -396,7 +426,7 @@
     for i in range(NX):
         earlier = earlier + jnp.where(i < x, tx_r[i], nothing)
     updated = anchor_ref[...] + (earlier + reached)
-    upd_ref[0] = updated
+    out_ref[:, 0:CHAN] = updated
     change = updated - lat_ref[0]
     er_s[...] = jnp.sum(change * change, axis=1)
     er_r[tok] = er_s[...]
@@ -407,8 +437,8 @@
     each(NT, lambda k: er_copy(k).start())
     each(NT, lambda k: er_copy(k).wait())
     summed = jnp.sum(jnp.sum(er_r[...], axis=0), axis=1, keepdims=True) * (1.0 / (CHAN * TOKENS))
-    spot = lax.broadcasted_iota(jnp.int32, (IMAGES, 128), 0) == lax.broadcasted_iota(jnp.int32, (IMAGES, 128), 1)
-    err_ref[...] = jnp.sum(jnp.where(spot, summed, 0.0), axis=0, keepdims=True)[:, 0:IMAGES]
+    for b in range(IMAGES):
+        out_ref[b, CHAN:8] = jnp.broadcast_to(summed[b : b + 1], (CHAN, 128))
 
 
 def body(
@@ -419,14 +449,11 @@
     vmem = pl.BlockSpec(memory_space=pltpu.VMEM)
     anywhere = pl.BlockSpec(memory_space=pl.ANY)
     dma = pltpu.SemaphoreType.DMA
-    updated, errors = pl.pallas_call(
+    result = pl.pallas_call(
         kernel,
-        out_shape=(
-            jax.ShapeDtypeStruct((1, IMAGES, CHAN, 128), F32),
-            jax.ShapeDtypeStruct((1, IMAGES), F32),
-        ),
+        out_shape=jax.ShapeDtypeStruct((IMAGES, 8, 128), F32),
         in_specs=[pl.BlockSpec(memory_space=pltpu.SMEM)] * 2 + [vmem] * 10 + [anywhere] * 3,
-        out_specs=(vmem, vmem),
+        out_specs=vmem,
         scratch_shapes=[
             pltpu.VMEM((FREQ, D), BF16),
             pltpu.VMEM((432, D), BF16),
@@ -455,7 +482,9 @@
             pltpu.VMEM((D, HALF), F32),
             pltpu.VMEM((IMAGES, NT, HP, 128), BF16),
             pltpu.VMEM((IMAGES, NT, HP, 128), BF16),
-            pltpu.VMEM((NZ, IMAGES, CHAN, 128), F32),
+            pltpu.VMEM((4, IMAGES, CHAN, 128), F32),
+            pltpu.VMEM((4, 2, IMAGES, CHAN, 128), F32),
+            pltpu.VMEM((4, 2, IMAGES, CHAN, 128), F32),
             pltpu.VMEM((NX, IMAGES, CHAN, 128), F32),
             pltpu.VMEM((NT, IMAGES, 128), F32),
             pltpu.VMEM((IMAGES, 128), F32),
@@ -463,14 +492,14 @@
             dma((3,)),
             dma((NT,)), dma((NT,)),
             dma((NT,)), dma((NT,)),
-            dma((NZ,)), dma((NZ,)),
-            dma((NZ,)), dma((NZ,)),
+            dma((8,)), dma((8,)),
+            dma((8,)), dma((8,)),
             dma((NX,)), dma((NX,)),
-            dma((NZ,)), dma((NZ,)),
+            dma((8,)), dma((8,)),
             dma((NX,)), dma((NX,)),
             dma, dma,
             dma((IMAGES, NT)), dma((IMAGES, NT)),
-            dma((NZ,)), dma((NZ,)),
+            dma((8,)), dma((8,)),
             dma((NX,)), dma((NX,)),
             dma((NT,)), dma((NT,)),
         ],
@@ -482,7 +511,7 @@
         slot_steps, class_labels, latents, anchor, noise_draws, freq, class_table, final_weight, in_weight, spread,
         qkv_weight, out_weight, time_weight, mod_weight.T, table,
     )
-    return updated, errors
+    return result[None, :, 0:CHAN], result[None, :, CHAN, 0]
 
 
 def solution(mesh):

time: 81 us -> 85.3 us (1.053)
  Pallas kernels: 77.7 us -> 81.6 us
    pallas_call x1, Pallas kernels: 77.7 us -> 81.6 us  [body(): pl.pallas_call(kernel, out_shape=jax.ShapeDtypeStruct((IMAGES, 8, 128), F...]
    unnamed x2 -> x0, local copies, waits for them, and re-layouts: 2.43 us -> none
    slice x0 -> x1, local copies, waits for them, and re-layouts: none -> 1.34 us  [body(): return (result[None, :, 0:CHAN], result[None, :, CHAN, 0])]
    broadcast_in_dim x0 -> x1, local copies, waits for them, and re-layouts: none -> 1.32 us  [body(): return (result[None, :, 0:CHAN], result[None, :, CHAN, 0])]
where the time goes in v3:
time: 85.3 us; the launch traced here: 84.9 us
  Pallas kernels  81.6 us (96%)
  local copies, waits for them, and re-layouts  2.66 us (3%)
    pallas_call x1, Pallas kernels, body(): pl.pallas_call(kernel, out_shape=jax.ShapeDtypeStruct((IMAGES, 8, 128), F...  81.6 us

profile of v3, /device:TPU:1, one launch (start us, length us, event | category | flops | bytes accessed | tf_op | source)
XLA Modules:
  0.0 84.9 jit_solution(10806044501903343996)
XLA Ops:
  0.6 81.6 %shard_map.158 = f32[4,8,128]{2,1,0:T(8,128)} custom-call(s32[1,2]{1,0:T(1,128)} %steps_ref.1, s32[4]{0:T(128)} %labels_ref.1, f32[1,4,4,128]{3,2,1,0:T(4,128)} %lat_ref.1, f32[4,4,128]{2,1,0:T(4,128)} %anchor_ref.1, f32[1,4,4,128]{3,2,1,0:T(4,128)} %noise_ref.1, f32[1,128]{1,0:T(1,128)} %constant.8.clone.freq_ref, bf16[1000,1152]{1,0:T(8,128)(2,1)} %cls_ref.1, ...), custom_call_target="tpu_custom_call" | custom-call | flops 6000000000 | bytes 8000000 | tf_op jit(solution)/shard_map/pallas_call | solution.py:452
  82.3 1.3 %slice_reduce_fusion = f32[4]{0:T(128)} fusion(f32[4,8,128]{2,1,0:T(8,128)} %shard_map.158), kind=kLoop, calls=%fused_computation.1 | loop fusion | bytes 32 | tf_op jit(solution)/shard_map/slice | solution.py:514
  83.6 1.3 %slice_bitcast_fusion = f32[1,4,4,128]{3,2,1,0:T(4,128)} fusion(f32[4,8,128]{2,1,0:T(8,128)} %shard_map.158), kind=kLoop, calls=%fused_computation | loop fusion | bytes 16384 | tf_op jit(solution)/shard_map/broadcast_in_dim | solution.py:514

commit v4 on v2

--- a/solution.py
+++ b/solution.py
@@ -78,8 +78,8 @@
     steps_ref, labels_ref, lat_ref, anchor_ref, noise_ref, freq_ref, cls_ref, fw_ref, inw_ref, spread_ref,
     wq_ref, wo_ref, time_hbm, mod_hbm, table_hbm,
     upd_ref, err_ref,
-    time_w, mod_w, table, tcat, xs, xo, psrc, pr, mod_s, mod_r, mod_t, rb, ab, shifts,
-    zw, zr, wf, wx, wt, zo, po, of, wob, emb, own, att_s, att_r,
+    time_w, mod_w, table, tcat, xs, xo, psrc, pr, mod_s, mod_r, gain_rows, gate_t, ab, shifts,
+    zw, zr, wf, wx, wt, zo, po, of, wob, wot, emb, own, query_s, key_s, value_s, att_s, att_r,
     dr_r, tx_r, er_r, er_s, invs,
     loc_sem, pr_send, pr_recv, mod_send, mod_recv, zw_send, zw_recv, zr_send, zr_recv,
     wx_send, wx_recv, zo_send, zo_recv, ox_send, ox_recv, sib_send, sib_recv,
@@ -143,12 +143,50 @@
             zw[z] = packed[0:16].astype(BF16)
             zr[z] = packed[16:18]
 
+    pl.semaphore_wait(barrier, NZ - 1 + NX - 1 + NT - 1 + NT)
+
+    def prior_copy(k):
+        return remote(psrc, pr.at[tok], pr_send.at[k], pr_recv.at[tok], (after, k))
+
+    def prior_arrival(k):
+        return remote(psrc, pr.at[k], pr_send.at[k], pr_recv.at[k], (after, k))
+
+    def zw_copy(k):
+        return remote(zw.at[z], zw.at[z], zw_send.at[k], zw_recv.at[k], z_peer(k))
+
+    def zr_copy(k):
+        return remote(zr.at[z], zr.at[z], zr_send.at[k], zr_recv.at[k], z_peer(k))
+
+    def zo_copy(k):
+        return remote(zo.at[z], zo.at[z], zo_send.at[k], zo_recv.at[k], z_peer(k))
+
+    def wx_copy(k):
+        return remote(wx.at[x], wx.at[x], wx_send.at[k], wx_recv.at[k], x_peer(k))
+
+    def ox_copy(k):
+        return remote(wob.at[core, x], wob.at[core, x], ox_send.at[k], ox_recv.at[k], x_peer(k))
+
+    def mod_copy(k):
+        return remote(mod_s, mod_r.at[tok], mod_send.at[k], mod_recv.at[k], t_peer(k))
+
+    def att_copy(b, k):
+        there = lax.rem(tok + k, NT)
+        return remote(att_s.at[b, there], att_r.at[b, tok], att_send.at[b, k], att_recv.at[b, k], t_peer(k))
+
+    def start_w(k):
+        zw_copy(k).start()
+        zr_copy(k).start()
+
+    each(NZ, start_w)
+    each(NT, lambda k: prior_copy(k).start(), first=0)
+
     grid = lax.broadcasted_iota(jnp.int32, (SIDE, TOKENS), 1)
     line = lax.broadcasted_iota(jnp.int32, (SIDE, TOKENS), 0)
     chosen = [jnp.where(line == (grid >> 5), 1.0, 0.0), jnp.where(line == (grid & 31), 1.0, 0.0)]
     chosen = jnp.concatenate(chosen + [jnp.zeros((64, TOKENS), F32)], axis=0).astype(BF16)
-    xs[0:128] = chosen
-    xs[128:256] = chosen
+    for b in range(IMAGES):
+        xs[b, 0:128] = chosen
+        xs[b, 128:256] = chosen
     po[...] = jnp.zeros((PIECE, 128), F32)
     for c in range(2):
 
@@ -160,44 +198,6 @@
                 po[CHUNK * i : CHUNK * i + CHUNK] = wide[:, 128 * k : 128 * k + 128]
 
     zo[z] = po[...].astype(BF16)
-    pl.semaphore_wait(barrier, NZ - 1 + NX - 1 + NT - 1 + NT)
-
-    def prior_copy(k):
-        return remote(psrc, pr.at[tok], pr_send.at[k], pr_recv.at[tok], (after, k))
-
-    def prior_arrival(k):
-        return remote(psrc, pr.at[k], pr_send.at[k], pr_recv.at[k], (after, k))
-
-    def zw_copy(k):
-        return remote(zw.at[z], zw.at[z], zw_send.at[k], zw_recv.at[k], z_peer(k))
-
-    def zr_copy(k):
-        return remote(zr.at[z], zr.at[z], zr_send.at[k], zr_recv.at[k], z_peer(k))
-
-    def zo_copy(k):
-        return remote(zo.at[z], zo.at[z], zo_send.at[k], zo_recv.at[k], z_peer(k))
-
-    def wx_copy(k):
-        return remote(wx.at[x], wx.at[x], wx_send.at[k], wx_recv.at[k], x_peer(k))
-
-    def ox_copy(k):
-        return remote(wob.at[core, x], wob.at[core, x], ox_send.at[k], ox_recv.at[k], x_peer(k))
-
-    def mod_copy(k):
-        return remote(mod_s, mod_r.at[tok], mod_send.at[k], mod_recv.at[k], t_peer(k))
-
-    def att_copy(b, k):
-        there = lax.rem(tok + k, NT)
-        return remote(att_s.at[b, there], att_r.at[b, tok], att_send.at[b, k], att_recv.at[b, k], t_peer(k))
-
-    each(NT, lambda k: prior_copy(k).start(), first=0)
-
-    def start_w(k):
-        zw_copy(k).start()
-        zr_copy(k).start()
-
-    each(NZ, start_w)
-
     t_from = jnp.full((1, 128), steps_ref[0, 0].astype(F32))
     t_to = jnp.full((1, 128), steps_ref[0, 1].astype(F32))
     phases = t_from * freq_ref[...]
@@ -237,28 +237,20 @@
     lane = lax.broadcasted_iota(jnp.int32, (8, 128), 1)
     cross = jnp.where(lane < 64, inner, 0.0)
     crosses = jnp.concatenate(list(split3(cross)) + [jnp.zeros((8, 128), F32)], axis=0).astype(BF16)
-    crosses = jnp.dot(crosses, xs[0:128], preferred_element_type=F32)
+    crosses = jnp.dot(crosses, chosen, preferred_element_type=F32)
     crosses = (crosses[0:8] + crosses[8:16] + crosses[16:24])[0:CHAN]
 
     each(NT, lambda k: mod_copy(k).wait())
-    for source in range(NT):
-        mod_t[source * 432 : source * 432 + 432] = jnp.transpose(mod_r[source])[0:432]
+    shift_rows = jnp.concatenate([mod_r[0][:, 0:432], mod_r[1][:, 0:432], mod_r[2][:, 0:288]], axis=1)
+    gain_rows[...] = 1.0 + jnp.concatenate(
+        [mod_r[2][:, 288:432], mod_r[3][:, 0:432], mod_r[4][:, 0:432], mod_r[5][:, 0:144]], axis=1
+    )
+    gates = jnp.concatenate([mod_r[5][:, 144:432], mod_r[6][:, 0:432], mod_r[7][:, 0:432]], axis=1)
+    shift_split = jnp.concatenate(split2(shift_rows), axis=0)
+    gates = jnp.transpose(gates)
+    for b in range(IMAGES):
+        gate_t[:, b * 128 : b * 128 + 128] = jnp.broadcast_to(gates[:, b : b + 1], (D, 128))
     rows = 128
-
-    def gains(r, carry):
-        here = pl.ds(pl.multiple_of(r * rows, rows), rows)
-        shift = mod_t[here]
-        gain = 1.0 + mod_t[pl.ds(pl.multiple_of(D + r * rows, rows), rows)]
-        lanes = lax.broadcasted_iota(jnp.int32, (rows, 128), 1)
-        base = table[here]
-        for b in range(IMAGES):
-            value = jnp.where(lanes == 72, shift[:, b : b + 1], gain[:, b : b + 1] * base)
-            high, low = split2(value)
-            rb[here, 256 * b : 256 * b + 128] = high
-            rb[here, 256 * b + 128 : 256 * b + 256] = low
-        return carry
-
-    lax.fori_loop(0, D // rows, gains, 0)
     each(NT, lambda k: prior_arrival(k).wait(), first=0)
 
     def place(b):
@@ -266,8 +258,8 @@
         high = line.astype(BF16).astype(F32)
         low = line - high
         nought = jnp.zeros((CHAN, TOKENS), F32)
-        xs[64:80] = jnp.concatenate([high, low, nought, nought], axis=0).astype(BF16)
-        xs[192:208] = jnp.concatenate([high, nought, nought, nought], axis=0).astype(BF16)
+        xs[b, 64:80] = jnp.concatenate([high, low, nought, nought], axis=0).astype(BF16)
+        xs[b, 192:208] = jnp.concatenate([high, nought, nought, nought], axis=0).astype(BF16)
         return line
 
     for b in range(IMAGES):
@@ -277,7 +269,7 @@
             squares = squares + inner[0:CHAN, 64 + c : 65 + c] * line[c : c + 1]
         variance = spread_ref[...] + jnp.sum(line * squares, axis=0, keepdims=True) * (1.0 / D)
         invs[b] = lax.rsqrt(jnp.maximum(variance, 0.0) + 1e-06)
-        xo[:, b * 128 : b * 128 + 128] = xs[:, pl.ds(pl.multiple_of(tok * 128, 128), 128)]
+        xo[:, b * 128 : b * 128 + 128] = xs[b, :, pl.ds(pl.multiple_of(tok * 128, 128), 128)]
 
     def arrive_w(k):
         zw_copy(k).wait()
@@ -293,68 +285,83 @@
     own[...] = jnp.dot(tcat[...], xo[...], preferred_element_type=F32)
     each(NX, lambda k: wx_copy(k).wait())
     wt[...] = jnp.transpose(wx[...].reshape(D, 256))
-    folded = jnp.dot(wt[...], rb[...], preferred_element_type=F32)
-    for b in range(IMAGES):
-        both = folded[:, 256 * b : 256 * b + 128] + folded[:, 256 * b + 128 : 256 * b + 256]
+    wide = wt[...].astype(F32)
+    moved = lax.dot_general(wt[...], shift_split, (((1,), (1,)), ((), ())), preferred_element_type=F32)
+    moved = moved[:, 0:8] + moved[:, 8:16]
+    for b in range(IMAGES):
+        both = jnp.concatenate(split2(wide * gain_rows[b : b + 1]), axis=0)
+        folded = jnp.dot(both, tcat[...], preferred_element_type=F32)
+        both = folded[0:256, 0:128] + folded[0:256, 128:256] + folded[256:512, 0:128]
         high, low = split2(both)
         ab[b, :, 0:128] = high
         ab[b, :, 128:256] = low
-        shifts[b] = jnp.broadcast_to(both[:, 72:73], (256, 128))
+        shifts[b] = jnp.broadcast_to(moved[:, b : b + 1], (256, 128))
 
     factor = math.log2(math.e) / math.sqrt(HEAD)
     block = 256
 
-    def attend(b, carry):
-        place(b)
+    share = remote(wob.at[core], wob.at[core], sib_send, sib_recv, (slot, sibling))
+    other = remote(wob.at[1 - core], wob.at[1 - core], sib_send, sib_recv, (slot, sibling))
+
+    def prepare(b):
         shift = jnp.concatenate([shifts[b]] * NT, axis=1)
-        qkv = jnp.dot(ab[b], xs[...], preferred_element_type=F32) * invs[b] + shift
-        queries = jnp.concatenate([qkv[0:HEAD], jnp.zeros((128 - HEAD, TOKENS), F32)], axis=0).astype(BF16)
-        keys = jnp.transpose(qkv[HEAD : HEAD + 128]).astype(BF16)
-        values = jnp.concatenate([qkv[2 * HEAD : 3 * HEAD], jnp.ones((8, TOKENS), F32)], axis=0).astype(BF16)
-        for i in range(TOKENS // block):
-            scores = jnp.dot(keys, queries[:, i * block : (i + 1) * block], preferred_element_type=F32)
-            weights = jnp.exp2(scores * factor).astype(BF16)
-            summed = jnp.dot(values, weights, preferred_element_type=F32)
-            out = (summed / summed[HEAD : HEAD + 1]).astype(BF16)
+        qkv = jnp.dot(ab[b], xs[b], preferred_element_type=F32) * invs[b] + shift
+        queries = jnp.concatenate([qkv[0:HEAD] * factor, jnp.zeros((128 - HEAD, TOKENS), F32)], axis=0)
+        query_s[b % 2] = queries.astype(BF16)
+        key_s[b % 2] = jnp.transpose(qkv[HEAD : HEAD + 128]).astype(BF16)
+        values = jnp.concatenate([qkv[2 * HEAD : 3 * HEAD], jnp.ones((8, TOKENS), F32)], axis=0)
+        value_s[b % 2] = values.astype(BF16)
+
+    def scores_of(b, i):
+        here = query_s[b % 2, :, i * block : (i + 1) * block]
+        return jnp.dot(key_s[b % 2], here, preferred_element_type=F32)
+
+    blocks = TOKENS // block
+    prepare(0)
+    for b in range(IMAGES):
+        scores = scores_of(b, 0)
+        for i in range(blocks):
+            following = scores_of(b, i + 1) if i + 1 < blocks else None
+            if i == 1 and b + 1 < IMAGES:
+                prepare(b + 1)
+            weights = jnp.exp2(scores).astype(BF16)
+            summed = jnp.dot(value_s[b % 2], weights, preferred_element_type=F32)
+            out = (summed * (1.0 / summed[HEAD : HEAD + 1])).astype(BF16)
             for t in range(2):
                 att_s[b, 2 * i + t] = out[:, t * 128 : t * 128 + 128]
+            scores = following
         att_r[b, tok] = att_s[b, tok]
         each(NT, lambda k: att_copy(b, k).start())
-        return carry
-
-    lax.fori_loop(0, 1, attend, 0)
-
-    each(NZ, lambda k: zo_copy(k).wait())
-    for i in range(NZ):
-        base = 9 * i + (HP - HEAD) * (i // 8)
-        piece = zo[i].astype(F32)
-        for k in range(5):
-            of[base : base + CHUNK, 128 * k : 128 * k + 128] = piece[CHUNK * k : CHUNK * k + CHUNK]
-    for h in range(2):
-        of[h * HP + HEAD : (h + 1) * HP] = jnp.zeros((HP - HEAD, 640), F32)
-    wob[core, x] = of[...].astype(BF16)
-    each(NX, lambda k: ox_copy(k).start())
-    lax.fori_loop(1, 4, attend, 0)
-    each(NX, lambda k: ox_copy(k).wait())
-    share = remote(wob.at[core], wob.at[core], sib_send, sib_recv, (slot, sibling))
-    share.start()
-    other = remote(wob.at[1 - core], wob.at[1 - core], sib_send, sib_recv, (slot, sibling))
-    each(NT, lambda k: [att_copy(b, k).wait() for b in range(IMAGES)])
+        if b == 0:
+                each(NZ, lambda k: zo_copy(k).wait())
+                for i in range(NZ):
+                    base = 9 * i + (HP - HEAD) * (i // 8)
+                    piece = zo[i].astype(F32)
+                    for k in range(5):
+                        of[base : base + CHUNK, 128 * k : 128 * k + 128] = piece[CHUNK * k : CHUNK * k + CHUNK]
+                for h in range(2):
+                    of[h * HP + HEAD : (h + 1) * HP] = jnp.zeros((HP - HEAD, 640), F32)
+                wob[core, x] = of[...].astype(BF16)
+                each(NX, lambda k: ox_copy(k).start())
+        if b == 2:
+            each(NX, lambda k: ox_copy(k).wait())
+            share.start()
+
     share.wait_send()
     other.wait_recv()
-
+    for h in range(2):
+        turned = jnp.transpose(wob[h].reshape(HEADS * HP, 640))
+        wot[640 * h : 640 * h + 640] = turned
+    each(NT, lambda k: [att_copy(b, k).wait() for b in range(IMAGES)])
     attended = jnp.concatenate([att_r[b].reshape(HEADS * HP, 128) for b in range(IMAGES)], axis=1)
-    contract = (((0,), (0,)), ((), ()))
-    emb[0:640] = lax.dot_general(wob[0].reshape(HEADS * HP, 640), attended, contract, preferred_element_type=F32)
-    emb[640:D] = lax.dot_general(wob[1].reshape(HEADS * HP, 640)[:, 0:512], attended, contract, preferred_element_type=F32)
+    emb[...] = jnp.dot(wot[0:D], attended, preferred_element_type=F32)
 
     def hidden(r, total):
         here = pl.ds(pl.multiple_of(r * rows, rows), rows)
-        gates = mod_t[pl.ds(pl.multiple_of(2 * D + r * rows, rows), rows)]
         sums = []
         for b in range(IMAGES):
             cut = slice(b * 128, b * 128 + 128)
-            value = own[here, cut] + gates[:, b : b + 1] * emb[here, cut]
+            value = own[here, cut] + gate_t[here, cut] * emb[here, cut]
             emb[here, cut] = value
             sums.append(jnp.sum(value.reshape(rows // 8, 8, 128), axis=0))
         return total + jnp.concatenate(sums, axis=1)
@@ -432,14 +439,14 @@
             pltpu.VMEM((432, D), BF16),
             pltpu.VMEM((D, 128), F32),
             pltpu.VMEM((D, 256), BF16),
-            pltpu.VMEM((256, TOKENS), BF16),
+            pltpu.VMEM((IMAGES, 256, TOKENS), BF16),
             pltpu.VMEM((256, HALF), BF16),
             pltpu.VMEM((IMAGES, CHAN, 128), F32),
             pltpu.VMEM((NT, IMAGES, CHAN, 128), F32),
             pltpu.VMEM((8, 512), F32),
             pltpu.VMEM((NT, 8, 512), F32),
-            pltpu.VMEM((3 * D, 8), F32),
-            pltpu.VMEM((D, 256 * IMAGES), BF16),
+            pltpu.VMEM((8, D), F32),
+            pltpu.VMEM((D, HALF), F32),
             pltpu.VMEM((IMAGES, 256, 256), BF16),
             pltpu.VMEM((IMAGES, 256, 128), F32),
             pltpu.VMEM((NZ, 16, 256), BF16),
@@ -451,8 +458,12 @@
             pltpu.VMEM((PIECE, 128), F32),
             pltpu.VMEM((2 * HP, 640), F32),
             pltpu.VMEM((2, NX, 2 * HP, 640), BF16),
+            pltpu.VMEM((1280, 640), BF16),
             pltpu.VMEM((D, HALF), F32),
             pltpu.VMEM((D, HALF), F32),
+            pltpu.VMEM((2, 128, TOKENS), BF16),
+            pltpu.VMEM((2, TOKENS, 128), BF16),
+            pltpu.VMEM((2, HP, TOKENS), BF16),
             pltpu.VMEM((IMAGES, NT, HP, 128), BF16),
             pltpu.VMEM((IMAGES, NT, HP, 128), BF16),
             pltpu.VMEM((NZ, IMAGES, CHAN, 128), F32),

time: 81 us -> 87 us (1.074)
  Pallas kernels: 77.7 us -> 83.7 us
    pallas_call x1, Pallas kernels: 77.7 us -> 83.7 us  [body(): pl.pallas_call(kernel, out_shape=(jax.ShapeDtypeStruct((1, IMAGES, CHAN,...]
where the time goes in v4:
time: 87 us; the launch traced here: 86.8 us
  Pallas kernels  83.7 us (96%)
  local copies, waits for them, and re-layouts  2.43 us (3%)
    pallas_call x1, Pallas kernels, body(): pl.pallas_call(kernel, out_shape=(jax.ShapeDtypeStruct((1, IMAGES, CHAN,...  83.7 us
    unnamed x2, local copies, waits for them, and re-layouts  2.43 us

profile of v4, /device:TPU:1, one launch (start us, length us, event | category | flops | bytes accessed | tf_op | source)
XLA Modules:
  0.0 86.8 jit_solution(18052544282035466273)
XLA Ops:
  0.6 83.7 %shard_map.158 = (f32[1,4,4,128]{3,2,1,0:T(4,128)}, f32[1,4]{1,0:T(1,128)}) custom-call(s32[1,2]{1,0:T(1,128)} %steps_ref.1, s32[4]{0:T(128)} %labels_ref.1, f32[1,4,4,128]{3,2,1,0:T(4,128)} %lat_ref.1, f32[4,4,128]{2,1,0:T(4,128)} %anchor_ref.1, f32[1,4,4,128]{3,2,1,0:T(4,128)} %noise_ref.1, f32[1,128]{1,0:T(1,128)} %constant.8.clone.freq_ref, ...), custom_call_target="tpu_custom_call" | custom-call | flops 6000000000 | bytes 8000000 | tf_op jit(solution)/shard_map/pallas_call | solution.py:429
  84.3 1.3 %copy.19 = f32[1,4,4,128]{3,2,1,0:T(4,128)} copy(f32[1,4,4,128]{3,2,1,0:T(4,128)} %get-tuple-element.4) | data formatting | bytes 16384
  85.6 1.1 %copy.20 = f32[1,4]{1,0:T(1,128)} copy(f32[1,4]{1,0:T(1,128)} %get-tuple-element.5) | data formatting | bytes 32

commit v5 on v4

--- a/solution.py
+++ b/solution.py
@@ -23,7 +23,6 @@
 SLOTS = NX * NZ
 HP = 80
 CHUNK = 9
-PIECE = 48
 HALF = 512
 F32 = jnp.float32
 BF16 = jnp.bfloat16
@@ -79,10 +78,10 @@
     wq_ref, wo_ref, time_hbm, mod_hbm, table_hbm,
     upd_ref, err_ref,
     time_w, mod_w, table, tcat, xs, xo, psrc, pr, mod_s, mod_r, gain_rows, gate_t, ab, shifts,
-    zw, zr, wf, wx, wt, zo, po, of, wob, wot, emb, own, query_s, key_s, value_s, att_s, att_r,
+    zw, zr, wf, wx, wt, zo, of, wob, w8, wot, emb, own, query_s, key_s, value_s, att_s, att_r,
     dr_r, tx_r, er_r, er_s, invs,
     loc_sem, pr_send, pr_recv, mod_send, mod_recv, zw_send, zw_recv, zr_send, zr_recv,
-    wx_send, wx_recv, zo_send, zo_recv, ox_send, ox_recv, sib_send, sib_recv,
+    wx_send, wx_recv, zo_send, zo_recv, ox_send, ox_recv, oy_send, oy_recv, sib_send, sib_recv,
     att_send, att_recv, dr_send, dr_recv, tx_send, tx_recv, er_send, er_recv,
 ):
     slot = lax.axis_index("tm")
@@ -143,6 +142,10 @@
             zw[z] = packed[0:16].astype(BF16)
             zr[z] = packed[16:18]
 
+    own_rows = wo_ref[:, pl.ds(pl.multiple_of(tok * 128, 128), 128)].astype(F32)
+    last_rows = wo_ref[:, 8 * 128 : 9 * 128].astype(F32)
+    last_rows = jnp.where(core == 0, last_rows[0:7], jnp.concatenate([last_rows[7:9], jnp.zeros((5, 128), F32)], axis=0))
+    zo[z] = jnp.concatenate([own_rows, last_rows], axis=0).astype(BF16)
     pl.semaphore_wait(barrier, NZ - 1 + NX - 1 + NT - 1 + NT)
 
     def prior_copy(k):
@@ -163,8 +166,29 @@
     def wx_copy(k):
         return remote(wx.at[x], wx.at[x], wx_send.at[k], wx_recv.at[k], x_peer(k))
 
-    def ox_copy(k):
-        return remote(wob.at[core, x], wob.at[core, x], ox_send.at[k], ox_recv.at[k], x_peer(k))
+    def ox_copies(k):
+        return [
+            remote(wob.at[tok, x], wob.at[tok, x], ox_send.at[k], ox_recv.at[k], x_peer(k)),
+            remote(w8.at[core, x], w8.at[core, x], ox_send.at[NX + k], ox_recv.at[NX + k], x_peer(k)),
+        ]
+
+    def oy_copy(k):
+        there = 2 * lax.rem(lax.div(tok, 2) + k, 4) + core
+        return remote(wob.at[tok], wob.at[tok], oy_send.at[k], oy_recv.at[k], (slot, there))
+
+    def share_copies(side):
+        return [
+            remote(wob.at[2 * q + side], wob.at[2 * q + side], sib_send.at[q], sib_recv.at[q], (slot, sibling))
+            for q in range(4)
+        ] + [remote(w8.at[side], w8.at[side], sib_send.at[4], sib_recv.at[4], (slot, sibling))]
+
+    def start(copies):
+        for copy in copies:
+            copy.start()
+
+    def finish(copies):
+        for copy in copies:
+            copy.wait()
 
     def mod_copy(k):
         return remote(mod_s, mod_r.at[tok], mod_send.at[k], mod_recv.at[k], t_peer(k))
@@ -179,6 +203,7 @@
 
     each(NZ, start_w)
     each(NT, lambda k: prior_copy(k).start(), first=0)
+    each(NZ, lambda k: zo_copy(k).start())
 
     grid = lax.broadcasted_iota(jnp.int32, (SIDE, TOKENS), 1)
     line = lax.broadcasted_iota(jnp.int32, (SIDE, TOKENS), 0)
@@ -187,17 +212,6 @@
     for b in range(IMAGES):
         xs[b, 0:128] = chosen
         xs[b, 128:256] = chosen
-    po[...] = jnp.zeros((PIECE, 128), F32)
-    for c in range(2):
-
-        @pl.when(core == c)
-        def _():
-            wide = wo_ref[...].astype(F32)
-            for i in range(5 - c):
-                k = 5 * c + i
-                po[CHUNK * i : CHUNK * i + CHUNK] = wide[:, 128 * k : 128 * k + 128]
-
-    zo[z] = po[...].astype(BF16)
     t_from = jnp.full((1, 128), steps_ref[0, 0].astype(F32))
     t_to = jnp.full((1, 128), steps_ref[0, 1].astype(F32))
     phases = t_from * freq_ref[...]
@@ -276,12 +290,31 @@
         zr_copy(k).wait()
 
     each(NZ, arrive_w)
-    each(NZ, lambda k: zo_copy(k).start())
     for i in range(NZ):
         wf[18 * i : 18 * i + 16] = zw[i].astype(F32)
         wf[18 * i + 16 : 18 * i + 18] = zr[i]
     wx[x] = wf[...].astype(BF16)
     each(NX, lambda k: wx_copy(k).start())
+    each(NZ, lambda k: zo_copy(k).wait())
+    of[...] = jnp.zeros((2, 2 * HP, 128), F32)
+    for i in range(NZ):
+        base = 9 * i + (HP - HEAD) * (i // 8)
+        of[0, base : base + CHUNK] = zo[i].astype(F32)[0:CHUNK]
+    for c in range(2):
+
+        @pl.when(core == c)
+        def _():
+            for i in range(NZ):
+                base = 9 * i + (HP - HEAD) * (i // 8)
+                piece = zo[i].astype(F32)
+                if c == 0:
+                    of[1, base : base + 7] = piece[9:16]
+                else:
+                    of[1, base + 7 : base + 9] = piece[9:11]
+
+    wob[tok, x] = of[0].astype(BF16)
+    w8[core, x] = of[1].astype(BF16)
+    each(NX, lambda k: start(ox_copies(k)))
     own[...] = jnp.dot(tcat[...], xo[...], preferred_element_type=F32)
     each(NX, lambda k: wx_copy(k).wait())
     wt[...] = jnp.transpose(wx[...].reshape(D, 256))
@@ -300,8 +333,8 @@
     factor = math.log2(math.e) / math.sqrt(HEAD)
     block = 256
 
-    share = remote(wob.at[core], wob.at[core], sib_send, sib_recv, (slot, sibling))
-    other = remote(wob.at[1 - core], wob.at[1 - core], sib_send, sib_recv, (slot, sibling))
+    each(NX, lambda k: finish(ox_copies(k)))
+    each(4, lambda k: oy_copy(k).start())
 
     def prepare(b):
         shift = jnp.concatenate([shifts[b]] * NT, axis=1)
@@ -332,29 +365,20 @@
             scores = following
         att_r[b, tok] = att_s[b, tok]
         each(NT, lambda k: att_copy(b, k).start())
-        if b == 0:
-                each(NZ, lambda k: zo_copy(k).wait())
-                for i in range(NZ):
-                    base = 9 * i + (HP - HEAD) * (i // 8)
-                    piece = zo[i].astype(F32)
-                    for k in range(5):
-                        of[base : base + CHUNK, 128 * k : 128 * k + 128] = piece[CHUNK * k : CHUNK * k + CHUNK]
-                for h in range(2):
-                    of[h * HP + HEAD : (h + 1) * HP] = jnp.zeros((HP - HEAD, 640), F32)
-                wob[core, x] = of[...].astype(BF16)
-                each(NX, lambda k: ox_copy(k).start())
         if b == 2:
-            each(NX, lambda k: ox_copy(k).wait())
-            share.start()
-
-    share.wait_send()
-    other.wait_recv()
-    for h in range(2):
-        turned = jnp.transpose(wob[h].reshape(HEADS * HP, 640))
-        wot[640 * h : 640 * h + 640] = turned
+            each(4, lambda k: oy_copy(k).wait())
+            start(share_copies(core))
+
+    for copy in share_copies(core):
+        copy.wait_send()
+    for copy in share_copies(1 - core):
+        copy.wait_recv()
+    for t in range(NT):
+        wot[128 * t : 128 * t + 128] = jnp.transpose(wob[t].reshape(HEADS * HP, 128))
+    wot[1024:D] = jnp.transpose((w8[0] + w8[1]).reshape(HEADS * HP, 128))
     each(NT, lambda k: [att_copy(b, k).wait() for b in range(IMAGES)])
     attended = jnp.concatenate([att_r[b].reshape(HEADS * HP, 128) for b in range(IMAGES)], axis=1)
-    emb[...] = jnp.dot(wot[0:D], attended, preferred_element_type=F32)
+    emb[...] = jnp.dot(wot[...], attended, preferred_element_type=F32)
 
     def hidden(r, total):
         here = pl.ds(pl.multiple_of(r * rows, rows), rows)
@@ -454,11 +478,11 @@
             pltpu.VMEM((18 * NZ, 256), F32),
             pltpu.VMEM((NX, 18 * NZ, 256), BF16),
             pltpu.VMEM((256, D), BF16),
-            pltpu.VMEM((NZ, PIECE, 128), BF16),
-            pltpu.VMEM((PIECE, 128), F32),
-            pltpu.VMEM((2 * HP, 640), F32),
-            pltpu.VMEM((2, NX, 2 * HP, 640), BF16),
-            pltpu.VMEM((1280, 640), BF16),
+            pltpu.VMEM((NZ, 16, 128), BF16),
+            pltpu.VMEM((2, 2 * HP, 128), F32),
+            pltpu.VMEM((NT, NX, 2 * HP, 128), BF16),
+            pltpu.VMEM((2, NX, 2 * HP, 128), BF16),
+            pltpu.VMEM((D, 640), BF16),
             pltpu.VMEM((D, HALF), F32),
             pltpu.VMEM((D, HALF), F32),
             pltpu.VMEM((2, 128, TOKENS), BF16),
@@ -478,8 +502,9 @@
             dma((NZ,)), dma((NZ,)),
             dma((NX,)), dma((NX,)),
             dma((NZ,)), dma((NZ,)),
-            dma((NX,)), dma((NX,)),
-            dma, dma,
+            dma((2 * NX,)), dma((2 * NX,)),
+            dma((4,)), dma((4,)),
+            dma((5,)), dma((5,)),
             dma((IMAGES, NT)), dma((IMAGES, NT)),
             dma((NZ,)), dma((NZ,)),
             dma((NX,)), dma((NX,)),

time: 87 us -> 86.2 us (level)
  no operation moved by 1% of the time
where the time goes in v5:
time: 86.2 us; the launch traced here: 86 us
  Pallas kernels  82.9 us (96%)
  local copies, waits for them, and re-layouts  2.43 us (3%)
    pallas_call x1, Pallas kernels, body(): pl.pallas_call(kernel, out_shape=(jax.ShapeDtypeStruct((1, IMAGES, CHAN,...  82.9 us
    unnamed x2, local copies, waits for them, and re-layouts  2.43 us

profile of v5, /device:TPU:1, one launch (start us, length us, event | category | flops | bytes accessed | tf_op | source)
XLA Modules:
  0.0 86.0 jit_solution(5971481683865467408)
XLA Ops:
  0.6 82.9 %shard_map.158 = (f32[1,4,4,128]{3,2,1,0:T(4,128)}, f32[1,4]{1,0:T(1,128)}) custom-call(s32[1,2]{1,0:T(1,128)} %steps_ref.1, s32[4]{0:T(128)} %labels_ref.1, f32[1,4,4,128]{3,2,1,0:T(4,128)} %lat_ref.1, f32[4,4,128]{2,1,0:T(4,128)} %anchor_ref.1, f32[1,4,4,128]{3,2,1,0:T(4,128)} %noise_ref.1, f32[1,128]{1,0:T(1,128)} %constant.8.clone.freq_ref, ...), custom_call_target="tpu_custom_call" | custom-call | flops 6000000000 | bytes 8000000 | tf_op jit(solution)/shard_map/pallas_call | solution.py:453
  83.5 1.3 %copy.19 = f32[1,4,4,128]{3,2,1,0:T(4,128)} copy(f32[1,4,4,128]{3,2,1,0:T(4,128)} %get-tuple-element.4) | data formatting | bytes 16384
  84.8 1.1 %copy.20 = f32[1,4]{1,0:T(1,128)} copy(f32[1,4]{1,0:T(1,128)} %get-tuple-element.5) | data formatting | bytes 32

commit v6 on v5

--- a/solution.py
+++ b/solution.py
@@ -77,8 +77,8 @@
     steps_ref, labels_ref, lat_ref, anchor_ref, noise_ref, freq_ref, cls_ref, fw_ref, inw_ref, spread_ref,
     wq_ref, wo_ref, time_hbm, mod_hbm, table_hbm,
     upd_ref, err_ref,
-    time_w, mod_w, table, tcat, xs, xo, psrc, pr, mod_s, mod_r, gain_rows, gate_t, ab, shifts,
-    zw, zr, wf, wx, wt, zo, of, wob, w8, wot, emb, own, query_s, key_s, value_s, att_s, att_r,
+    time_w, mod_w, table, tcat, xs, xo, psrc, pr, mod_s, mod_r, mod_t, rb, gate_t, ab, shifts,
+    zw, zr, wf, wx, wt, zo, of, wob, w8, wot, emb, own, att_s, att_r,
     dr_r, tx_r, er_r, er_s, invs,
     loc_sem, pr_send, pr_recv, mod_send, mod_recv, zw_send, zw_recv, zr_send, zr_recv,
     wx_send, wx_recv, zo_send, zo_recv, ox_send, ox_recv, oy_send, oy_recv, sib_send, sib_recv,
@@ -101,11 +101,8 @@
         return (slot, lax.rem(tok + k, NT))
 
     def each(count, action, first=1):
-        def step(k, carry):
+        for k in range(first, count):
             action(k)
-            return carry
-
-        lax.fori_loop(first, count, step, 0)
 
     def remote(src, dst, send, recv, device):
         return pltpu.make_async_remote_copy(
@@ -255,16 +252,20 @@
     crosses = (crosses[0:8] + crosses[8:16] + crosses[16:24])[0:CHAN]
 
     each(NT, lambda k: mod_copy(k).wait())
-    shift_rows = jnp.concatenate([mod_r[0][:, 0:432], mod_r[1][:, 0:432], mod_r[2][:, 0:288]], axis=1)
-    gain_rows[...] = 1.0 + jnp.concatenate(
-        [mod_r[2][:, 288:432], mod_r[3][:, 0:432], mod_r[4][:, 0:432], mod_r[5][:, 0:144]], axis=1
-    )
-    gates = jnp.concatenate([mod_r[5][:, 144:432], mod_r[6][:, 0:432], mod_r[7][:, 0:432]], axis=1)
-    shift_split = jnp.concatenate(split2(shift_rows), axis=0)
-    gates = jnp.transpose(gates)
-    for b in range(IMAGES):
-        gate_t[:, b * 128 : b * 128 + 128] = jnp.broadcast_to(gates[:, b : b + 1], (D, 128))
+    for source in range(NT):
+        mod_t[source * 432 : source * 432 + 432] = jnp.transpose(mod_r[source])[0:432]
     rows = 128
+    lanes = lax.broadcasted_iota(jnp.int32, (rows, 128), 1)
+    for r in range(D // rows):
+        here = slice(r * rows, r * rows + rows)
+        shift = mod_t[r * rows : r * rows + rows]
+        gain = 1.0 + mod_t[D + r * rows : D + r * rows + rows]
+        base = table[here]
+        for b in range(IMAGES):
+            value = jnp.where(lanes == 72, shift[:, b : b + 1], gain[:, b : b + 1] * base)
+            high, low = split2(value)
+            rb[here, 256 * b : 256 * b + 128] = high
+            rb[here, 256 * b + 128 : 256 * b + 256] = low
     each(NT, lambda k: prior_arrival(k).wait(), first=0)
 
     def place(b):
@@ -316,19 +317,19 @@
     w8[core, x] = of[1].astype(BF16)
     each(NX, lambda k: start(ox_copies(k)))
     own[...] = jnp.dot(tcat[...], xo[...], preferred_element_type=F32)
+    for r in range(D // rows):
+        gate = mod_t[2 * D + r * rows : 2 * D + r * rows + rows]
+        for b in range(IMAGES):
+            gate_t[r * rows : r * rows + rows, b * 128 : b * 128 + 128] = jnp.broadcast_to(gate[:, b : b + 1], (rows, 128))
     each(NX, lambda k: wx_copy(k).wait())
     wt[...] = jnp.transpose(wx[...].reshape(D, 256))
-    wide = wt[...].astype(F32)
-    moved = lax.dot_general(wt[...], shift_split, (((1,), (1,)), ((), ())), preferred_element_type=F32)
-    moved = moved[:, 0:8] + moved[:, 8:16]
+    folded = jnp.dot(wt[...], rb[...], preferred_element_type=F32)
     for b in range(IMAGES):
-        both = jnp.concatenate(split2(wide * gain_rows[b : b + 1]), axis=0)
-        folded = jnp.dot(both, tcat[...], preferred_element_type=F32)
-        both = folded[0:256, 0:128] + folded[0:256, 128:256] + folded[256:512, 0:128]
+        both = folded[:, 256 * b : 256 * b + 128] + folded[:, 256 * b + 128 : 256 * b + 256]
         high, low = split2(both)
         ab[b, :, 0:128] = high
         ab[b, :, 128:256] = low
-        shifts[b] = jnp.broadcast_to(moved[:, b : b + 1], (256, 128))
+        shifts[b] = jnp.broadcast_to(both[:, 72:73], (256, 128))
 
     factor = math.log2(math.e) / math.sqrt(HEAD)
     block = 256
@@ -336,39 +337,27 @@
     each(NX, lambda k: finish(ox_copies(k)))
     each(4, lambda k: oy_copy(k).start())
 
-    def prepare(b):
+    def attend(b, carry):
         shift = jnp.concatenate([shifts[b]] * NT, axis=1)
         qkv = jnp.dot(ab[b], xs[b], preferred_element_type=F32) * invs[b] + shift
-        queries = jnp.concatenate([qkv[0:HEAD] * factor, jnp.zeros((128 - HEAD, TOKENS), F32)], axis=0)
-        query_s[b % 2] = queries.astype(BF16)
-        key_s[b % 2] = jnp.transpose(qkv[HEAD : HEAD + 128]).astype(BF16)
-        values = jnp.concatenate([qkv[2 * HEAD : 3 * HEAD], jnp.ones((8, TOKENS), F32)], axis=0)
-        value_s[b % 2] = values.astype(BF16)
-
-    def scores_of(b, i):
-        here = query_s[b % 2, :, i * block : (i + 1) * block]
-        return jnp.dot(key_s[b % 2], here, preferred_element_type=F32)
-
-    blocks = TOKENS // block
-    prepare(0)
-    for b in range(IMAGES):
-        scores = scores_of(b, 0)
-        for i in range(blocks):
-            following = scores_of(b, i + 1) if i + 1 < blocks else None
-            if i == 1 and b + 1 < IMAGES:
-                prepare(b + 1)
+        queries = jnp.concatenate([qkv[0:HEAD] * factor, jnp.zeros((128 - HEAD, TOKENS), F32)], axis=0).astype(BF16)
+        keys = jnp.transpose(qkv[HEAD : HEAD + 128]).astype(BF16)
+        values = jnp.concatenate([qkv[2 * HEAD : 3 * HEAD], jnp.ones((8, TOKENS), F32)], axis=0).astype(BF16)
+        for i in range(TOKENS // block):
+            scores = jnp.dot(keys, queries[:, i * block : (i + 1) * block], preferred_element_type=F32)
             weights = jnp.exp2(scores).astype(BF16)
-            summed = jnp.dot(value_s[b % 2], weights, preferred_element_type=F32)
+            summed = jnp.dot(values, weights, preferred_element_type=F32)
             out = (summed * (1.0 / summed[HEAD : HEAD + 1])).astype(BF16)
             for t in range(2):
                 att_s[b, 2 * i + t] = out[:, t * 128 : t * 128 + 128]
-            scores = following
         att_r[b, tok] = att_s[b, tok]
         each(NT, lambda k: att_copy(b, k).start())
-        if b == 2:
-            each(4, lambda k: oy_copy(k).wait())
-            start(share_copies(core))
-
+        return carry
+
+    lax.fori_loop(0, 1, attend, 0)
+    each(4, lambda k: oy_copy(k).wait())
+    start(share_copies(core))
+    lax.fori_loop(1, IMAGES, attend, 0)
     for copy in share_copies(core):
         copy.wait_send()
     for copy in share_copies(1 - core):
@@ -380,24 +369,17 @@
     attended = jnp.concatenate([att_r[b].reshape(HEADS * HP, 128) for b in range(IMAGES)], axis=1)
     emb[...] = jnp.dot(wot[...], attended, preferred_element_type=F32)
 
-    def hidden(r, total):
-        here = pl.ds(pl.multiple_of(r * rows, rows), rows)
-        sums = []
-        for b in range(IMAGES):
-            cut = slice(b * 128, b * 128 + 128)
-            value = own[here, cut] + gate_t[here, cut] * emb[here, cut]
-            emb[here, cut] = value
-            sums.append(jnp.sum(value.reshape(rows // 8, 8, 128), axis=0))
-        return total + jnp.concatenate(sums, axis=1)
-
-    total = lax.fori_loop(0, D // rows, hidden, jnp.zeros((8, HALF), F32))
+    total = jnp.zeros((8, HALF), F32)
+    for r in range(D // rows):
+        here = slice(r * rows, r * rows + rows)
+        value = own[here] + gate_t[here] * emb[here]
+        emb[here] = value
+        total = total + jnp.sum(value.reshape(rows // 8, 8, HALF), axis=0)
     mean = jnp.sum(total, axis=0, keepdims=True) * (1.0 / D)
-
-    def square(r, total):
-        chunk = emb[pl.ds(pl.multiple_of(r * rows, rows), rows)] - mean
-        return total + jnp.sum((chunk * chunk).reshape(rows // 8, 8, HALF), axis=0)
-
-    total = lax.fori_loop(0, D // rows, square, jnp.zeros((8, HALF), F32))
+    total = jnp.zeros((8, HALF), F32)
+    for r in range(D // rows):
+        chunk = emb[r * rows : r * rows + rows] - mean
+        total = total + jnp.sum((chunk * chunk).reshape(rows // 8, 8, HALF), axis=0)
     inverse = lax.rsqrt(jnp.sum(total, axis=0, keepdims=True) * (1.0 / D) + 1e-06)
     final = ((emb[...] - mean) * inverse).astype(BF16)
     predicted = jnp.dot(fw_ref[...], final, preferred_element_type=F32)
@@ -469,7 +451,8 @@
             pltpu.VMEM((NT, IMAGES, CHAN, 128), F32),
             pltpu.VMEM((8, 512), F32),
             pltpu.VMEM((NT, 8, 512), F32),
-            pltpu.VMEM((8, D), F32),
+            pltpu.VMEM((3 * D, 8), F32),
+            pltpu.VMEM((D, 256 * IMAGES), BF16),
             pltpu.VMEM((D, HALF), F32),
             pltpu.VMEM((IMAGES, 256, 256), BF16),
             pltpu.VMEM((IMAGES, 256, 128), F32),
@@ -485,9 +468,6 @@
             pltpu.VMEM((D, 640), BF16),
             pltpu.VMEM((D, HALF), F32),
             pltpu.VMEM((D, HALF), F32),
-            pltpu.VMEM((2, 128, TOKENS), BF16),
-            pltpu.VMEM((2, TOKENS, 128), BF16),
-            pltpu.VMEM((2, HP, TOKENS), BF16),
             pltpu.VMEM((IMAGES, NT, HP, 128), BF16),
             pltpu.VMEM((IMAGES, NT, HP, 128), BF16),
             pltpu.VMEM((NZ, IMAGES, CHAN, 128), F32),

time: 86.2 us -> 89 us (1.032)
  Pallas kernels: 82.9 us -> 85.7 us
    pallas_call x1, Pallas kernels: 82.9 us -> 85.7 us  [body(): pl.pallas_call(kernel, out_shape=(jax.ShapeDtypeStruct((1, IMAGES, CHAN,...]
where the time goes in v6:
time: 89 us; the launch traced here: 88.8 us
  Pallas kernels  85.7 us (96%)
  local copies, waits for them, and re-layouts  2.43 us (3%)
    pallas_call x1, Pallas kernels, body(): pl.pallas_call(kernel, out_shape=(jax.ShapeDtypeStruct((1, IMAGES, CHAN,...  85.7 us
    unnamed x2, local copies, waits for them, and re-layouts  2.43 us

profile of v6, /device:TPU:1, one launch (start us, length us, event | category | flops | bytes accessed | tf_op | source)
XLA Modules:
  0.0 88.8 jit_solution(6074544631775444579)
XLA Ops:
  0.6 85.7 %shard_map.158 = (f32[1,4,4,128]{3,2,1,0:T(4,128)}, f32[1,4]{1,0:T(1,128)}) custom-call(s32[1,2]{1,0:T(1,128)} %steps_ref.1, s32[4]{0:T(128)} %labels_ref.1, f32[1,4,4,128]{3,2,1,0:T(4,128)} %lat_ref.1, f32[4,4,128]{2,1,0:T(4,128)} %anchor_ref.1, f32[1,4,4,128]{3,2,1,0:T(4,128)} %noise_ref.1, f32[1,128]{1,0:T(1,128)} %constant.8.clone.freq_ref, ...), custom_call_target="tpu_custom_call" | custom-call | flops 6000000000 | bytes 8000000 | tf_op jit(solution)/shard_map/pallas_call | solution.py:435
  86.3 1.3 %copy.19 = f32[1,4,4,128]{3,2,1,0:T(4,128)} copy(f32[1,4,4,128]{3,2,1,0:T(4,128)} %get-tuple-element.4) | data formatting | bytes 16384
  87.6 1.1 %copy.20 = f32[1,4]{1,0:T(1,128)} copy(f32[1,4]{1,0:T(1,128)} %get-tuple-element.5) | data formatting | bytes 32

commit v7 on v6

--- a/solution.py
+++ b/solution.py
@@ -78,8 +78,8 @@
     wq_ref, wo_ref, time_hbm, mod_hbm, table_hbm,
     upd_ref, err_ref,
     time_w, mod_w, table, tcat, xs, xo, psrc, pr, mod_s, mod_r, mod_t, rb, gate_t, ab, shifts,
-    zw, zr, wf, wx, wt, zo, of, wob, w8, wot, emb, own, att_s, att_r,
-    dr_r, tx_r, er_r, er_s, invs,
+    zw, zr, wf, wx, zo, of, wob, w8, emb, own, query_s, key_s, value_s, att_s, att_r,
+    dr_r, tx_r, er_r, er_s, invs, coef,
     loc_sem, pr_send, pr_recv, mod_send, mod_recv, zw_send, zw_recv, zr_send, zr_recv,
     wx_send, wx_recv, zo_send, zo_recv, ox_send, ox_recv, oy_send, oy_recv, sib_send, sib_recv,
     att_send, att_recv, dr_send, dr_recv, tx_send, tx_recv, er_send, er_recv,
@@ -232,6 +232,8 @@
     )
     mod_r[tok] = mod_s[...]
     each(NT, lambda k: mod_copy(k).start())
+    for i, value in enumerate(coefficients(t_from, t_to)):
+        coef[i : i + 1] = value
 
     loads[2].wait()
     inw = inw_ref[...].astype(F32)
@@ -322,8 +324,9 @@
         for b in range(IMAGES):
             gate_t[r * rows : r * rows + rows, b * 128 : b * 128 + 128] = jnp.broadcast_to(gate[:, b : b + 1], (rows, 128))
     each(NX, lambda k: wx_copy(k).wait())
-    wt[...] = jnp.transpose(wx[...].reshape(D, 256))
-    folded = jnp.dot(wt[...], rb[...], preferred_element_type=F32)
+    folded = lax.dot_general(
+        wx[...].reshape(D, 256), rb[...], (((0,), (0,)), ((), ())), preferred_element_type=F32
+    )
     for b in range(IMAGES):
         both = folded[:, 256 * b : 256 * b + 128] + folded[:, 256 * b + 128 : 256 * b + 256]
         high, low = split2(both)
@@ -337,37 +340,49 @@
     each(NX, lambda k: finish(ox_copies(k)))
     each(4, lambda k: oy_copy(k).start())
 
-    def attend(b, carry):
+    def prepare(b):
         shift = jnp.concatenate([shifts[b]] * NT, axis=1)
         qkv = jnp.dot(ab[b], xs[b], preferred_element_type=F32) * invs[b] + shift
-        queries = jnp.concatenate([qkv[0:HEAD] * factor, jnp.zeros((128 - HEAD, TOKENS), F32)], axis=0).astype(BF16)
-        keys = jnp.transpose(qkv[HEAD : HEAD + 128]).astype(BF16)
-        values = jnp.concatenate([qkv[2 * HEAD : 3 * HEAD], jnp.ones((8, TOKENS), F32)], axis=0).astype(BF16)
-        for i in range(TOKENS // block):
-            scores = jnp.dot(keys, queries[:, i * block : (i + 1) * block], preferred_element_type=F32)
+        queries = jnp.concatenate([qkv[0:HEAD] * factor, jnp.zeros((128 - HEAD, TOKENS), F32)], axis=0)
+        query_s[b % 2] = queries.astype(BF16)
+        key_s[b % 2] = jnp.transpose(qkv[HEAD : HEAD + 128]).astype(BF16)
+        values = jnp.concatenate([qkv[2 * HEAD : 3 * HEAD], jnp.ones((8, TOKENS), F32)], axis=0)
+        value_s[b % 2] = values.astype(BF16)
+
+    def scores_of(b, i):
+        here = query_s[b % 2, :, i * block : (i + 1) * block]
+        return jnp.dot(key_s[b % 2], here, preferred_element_type=F32)
+
+    blocks = TOKENS // block
+    prepare(0)
+    for b in range(IMAGES):
+        scores = scores_of(b, 0)
+        for i in range(blocks):
+            following = scores_of(b, i + 1) if i + 1 < blocks else None
+            if i == 1 and b + 1 < IMAGES:
+                prepare(b + 1)
             weights = jnp.exp2(scores).astype(BF16)
-            summed = jnp.dot(values, weights, preferred_element_type=F32)
+            summed = jnp.dot(value_s[b % 2], weights, preferred_element_type=F32)
             out = (summed * (1.0 / summed[HEAD : HEAD + 1])).astype(BF16)
             for t in range(2):
                 att_s[b, 2 * i + t] = out[:, t * 128 : t * 128 + 128]
+            scores = following
         att_r[b, tok] = att_s[b, tok]
         each(NT, lambda k: att_copy(b, k).start())
-        return carry
-
-    lax.fori_loop(0, 1, attend, 0)
-    each(4, lambda k: oy_copy(k).wait())
-    start(share_copies(core))
-    lax.fori_loop(1, IMAGES, attend, 0)
+        if b == 2:
+            each(4, lambda k: oy_copy(k).wait())
+            start(share_copies(core))
+
     for copy in share_copies(core):
         copy.wait_send()
     for copy in share_copies(1 - core):
         copy.wait_recv()
-    for t in range(NT):
-        wot[128 * t : 128 * t + 128] = jnp.transpose(wob[t].reshape(HEADS * HP, 128))
-    wot[1024:D] = jnp.transpose((w8[0] + w8[1]).reshape(HEADS * HP, 128))
     each(NT, lambda k: [att_copy(b, k).wait() for b in range(IMAGES)])
     attended = jnp.concatenate([att_r[b].reshape(HEADS * HP, 128) for b in range(IMAGES)], axis=1)
-    emb[...] = jnp.dot(wot[...], attended, preferred_element_type=F32)
+    columns = [wob[t].reshape(HEADS * HP, 128) for t in range(NT)] + [(w8[0] + w8[1]).reshape(HEADS * HP, 128)]
+    emb[...] = lax.dot_general(
+        jnp.concatenate(columns, axis=1), attended, (((0,), (0,)), ((), ())), preferred_element_type=F32
+    )
 
     total = jnp.zeros((8, HALF), F32)
     for r in range(D // rows):
@@ -384,7 +399,7 @@
     final = ((emb[...] - mean) * inverse).astype(BF16)
     predicted = jnp.dot(fw_ref[...], final, preferred_element_type=F32)
 
-    keep, noise, eps = coefficients(t_from, t_to)
+    keep, noise, eps = coef[0:1], coef[1:2], coef[2:3]
     for b in range(IMAGES):
         dr_r[z, b] = (keep - 1.0) * pr[tok, b] + eps * predicted[0:CHAN, b * 128 : b * 128 + 128] + noise * noise_ref[0, b]
 
@@ -460,14 +475,15 @@
             pltpu.VMEM((NZ, 2, 256), F32),
             pltpu.VMEM((18 * NZ, 256), F32),
             pltpu.VMEM((NX, 18 * NZ, 256), BF16),
-            pltpu.VMEM((256, D), BF16),
             pltpu.VMEM((NZ, 16, 128), BF16),
             pltpu.VMEM((2, 2 * HP, 128), F32),
             pltpu.VMEM((NT, NX, 2 * HP, 128), BF16),
             pltpu.VMEM((2, NX, 2 * HP, 128), BF16),
-            pltpu.VMEM((D, 640), BF16),
             pltpu.VMEM((D, HALF), F32),
             pltpu.VMEM((D, HALF), F32),
+            pltpu.VMEM((2, 128, TOKENS), BF16),
+            pltpu.VMEM((2, TOKENS, 128), BF16),
+            pltpu.VMEM((2, HP, TOKENS), BF16),
             pltpu.VMEM((IMAGES, NT, HP, 128), BF16),
             pltpu.VMEM((IMAGES, NT, HP, 128), BF16),
             pltpu.VMEM((NZ, IMAGES, CHAN, 128), F32),
@@ -475,6 +491,7 @@
             pltpu.VMEM((NT, IMAGES, 128), F32),
             pltpu.VMEM((IMAGES, 128), F32),
             pltpu.VMEM((IMAGES, 1, TOKENS), F32),
+            pltpu.VMEM((8, 128), F32),
             dma((3,)),
             dma((NT,)), dma((NT,)),
             dma((NT,)), dma((NT,)),

time: 89 us -> 85.8 us (0.964)
  Pallas kernels: 85.7 us -> 82.5 us
    pallas_call x1, Pallas kernels: 85.7 us -> 82.5 us  [body(): pl.pallas_call(kernel, out_shape=(jax.ShapeDtypeStruct((1, IMAGES, CHAN,...]
where the time goes in v7:
time: 85.8 us; the launch traced here: 85.6 us
  Pallas kernels  82.5 us (96%)
  local copies, waits for them, and re-layouts  2.43 us (3%)
    pallas_call x1, Pallas kernels, body(): pl.pallas_call(kernel, out_shape=(jax.ShapeDtypeStruct((1, IMAGES, CHAN,...  82.5 us
    unnamed x2, local copies, waits for them, and re-layouts  2.43 us

profile of v7, /device:TPU:1, one launch (start us, length us, event | category | flops | bytes accessed | tf_op | source)
XLA Modules:
  0.0 85.6 jit_solution(9567189643636012201)
XLA Ops:
  0.6 82.5 %shard_map.158 = (f32[1,4,4,128]{3,2,1,0:T(4,128)}, f32[1,4]{1,0:T(1,128)}) custom-call(s32[1,2]{1,0:T(1,128)} %steps_ref.1, s32[4]{0:T(128)} %labels_ref.1, f32[1,4,4,128]{3,2,1,0:T(4,128)} %lat_ref.1, f32[4,4,128]{2,1,0:T(4,128)} %anchor_ref.1, f32[1,4,4,128]{3,2,1,0:T(4,128)} %noise_ref.1, f32[1,128]{1,0:T(1,128)} %constant.8.clone.freq_ref, ...), custom_call_target="tpu_custom_call" | custom-call | flops 6000000000 | bytes 8000000 | tf_op jit(solution)/shard_map/pallas_call | solution.py:450
  83.1 1.3 %copy.19 = f32[1,4,4,128]{3,2,1,0:T(4,128)} copy(f32[1,4,4,128]{3,2,1,0:T(4,128)} %get-tuple-element.4) | data formatting | bytes 16384
  84.4 1.1 %copy.20 = f32[1,4]{1,0:T(1,128)} copy(f32[1,4]{1,0:T(1,128)} %get-tuple-element.5) | data formatting | bytes 32

commit v8 on v2

--- a/solution.py
+++ b/solution.py
@@ -79,8 +79,8 @@
     wq_ref, wo_ref, time_hbm, mod_hbm, table_hbm,
     upd_ref, err_ref,
     time_w, mod_w, table, tcat, xs, xo, psrc, pr, mod_s, mod_r, mod_t, rb, ab, shifts,
-    zw, zr, wf, wx, wt, zo, po, of, wob, emb, own, att_s, att_r,
-    dr_r, tx_r, er_r, er_s, invs,
+    zw, zr, wf, wx, zo, po, of, wob, emb, own, att_s, att_r,
+    dr_r, tx_r, er_r, er_s, invs, coef,
     loc_sem, pr_send, pr_recv, mod_send, mod_recv, zw_send, zw_recv, zr_send, zr_recv,
     wx_send, wx_recv, zo_send, zo_recv, ox_send, ox_recv, sib_send, sib_recv,
     att_send, att_recv, dr_send, dr_recv, tx_send, tx_recv, er_send, er_recv,
@@ -221,6 +221,8 @@
     )
     mod_r[tok] = mod_s[...]
     each(NT, lambda k: mod_copy(k).start())
+    for i, value in enumerate(coefficients(t_from, t_to)):
+        coef[i : i + 1] = value
 
     loads[2].wait()
     inw = inw_ref[...].astype(F32)
@@ -292,8 +294,9 @@
     each(NX, lambda k: wx_copy(k).start())
     own[...] = jnp.dot(tcat[...], xo[...], preferred_element_type=F32)
     each(NX, lambda k: wx_copy(k).wait())
-    wt[...] = jnp.transpose(wx[...].reshape(D, 256))
-    folded = jnp.dot(wt[...], rb[...], preferred_element_type=F32)
+    folded = lax.dot_general(
+        wx[...].reshape(D, 256), rb[...], (((0,), (0,)), ((), ())), preferred_element_type=F32
+    )
     for b in range(IMAGES):
         both = folded[:, 256 * b : 256 * b + 128] + folded[:, 256 * b + 128 : 256 * b + 256]
         high, low = split2(both)
@@ -305,6 +308,19 @@
     block = 256
 
     def attend(b, carry):
+        @pl.when(b == 1)
+        def _():
+            each(NZ, lambda k: zo_copy(k).wait())
+            for i in range(NZ):
+                base = 9 * i + (HP - HEAD) * (i // 8)
+                piece = zo[i].astype(F32)
+                for k in range(5):
+                    of[base : base + CHUNK, 128 * k : 128 * k + 128] = piece[CHUNK * k : CHUNK * k + CHUNK]
+            for h in range(2):
+                of[h * HP + HEAD : (h + 1) * HP] = jnp.zeros((HP - HEAD, 640), F32)
+            wob[core, x] = of[...].astype(BF16)
+            each(NX, lambda k: ox_copy(k).start())
+
         place(b)
         shift = jnp.concatenate([shifts[b]] * NT, axis=1)
         qkv = jnp.dot(ab[b], xs[...], preferred_element_type=F32) * invs[b] + shift
@@ -322,19 +338,7 @@
         each(NT, lambda k: att_copy(b, k).start())
         return carry
 
-    lax.fori_loop(0, 1, attend, 0)
-
-    each(NZ, lambda k: zo_copy(k).wait())
-    for i in range(NZ):
-        base = 9 * i + (HP - HEAD) * (i // 8)
-        piece = zo[i].astype(F32)
-        for k in range(5):
-            of[base : base + CHUNK, 128 * k : 128 * k + 128] = piece[CHUNK * k : CHUNK * k + CHUNK]
-    for h in range(2):
-        of[h * HP + HEAD : (h + 1) * HP] = jnp.zeros((HP - HEAD, 640), F32)
-    wob[core, x] = of[...].astype(BF16)
-    each(NX, lambda k: ox_copy(k).start())
-    lax.fori_loop(1, 4, attend, 0)
+    lax.fori_loop(0, IMAGES, attend, 0)
     each(NX, lambda k: ox_copy(k).wait())
     share = remote(wob.at[core], wob.at[core], sib_send, sib_recv, (slot, sibling))
     share.start()
@@ -371,7 +375,7 @@
     final = ((emb[...] - mean) * inverse).astype(BF16)
     predicted = jnp.dot(fw_ref[...], final, preferred_element_type=F32)
 
-    keep, noise, eps = coefficients(t_from, t_to)
+    keep, noise, eps = coef[0:1], coef[1:2], coef[2:3]
     for b in range(IMAGES):
         dr_r[z, b] = (keep - 1.0) * pr[tok, b] + eps * predicted[0:CHAN, b * 128 : b * 128 + 128] + noise * noise_ref[0, b]
 
@@ -446,7 +450,6 @@
             pltpu.VMEM((NZ, 2, 256), F32),
             pltpu.VMEM((18 * NZ, 256), F32),
             pltpu.VMEM((NX, 18 * NZ, 256), BF16),
-            pltpu.VMEM((256, D), BF16),
             pltpu.VMEM((NZ, PIECE, 128), BF16),
             pltpu.VMEM((PIECE, 128), F32),
             pltpu.VMEM((2 * HP, 640), F32),
@@ -460,6 +463,7 @@
             pltpu.VMEM((NT, IMAGES, 128), F32),
             pltpu.VMEM((IMAGES, 128), F32),
             pltpu.VMEM((IMAGES, 1, TOKENS), F32),
+            pltpu.VMEM((8, 128), F32),
             dma((3,)),
             dma((NT,)), dma((NT,)),
             dma((NT,)), dma((NT,)),

time: 81 us -> 80.9 us (level)
  no operation moved by 1% of the time
where the time goes in v8:
time: 80.9 us; the launch traced here: 80.7 us
  Pallas kernels  77.7 us (96%)
  local copies, waits for them, and re-layouts  2.43 us (3%)
    pallas_call x1, Pallas kernels, body(): pl.pallas_call(kernel, out_shape=(jax.ShapeDtypeStruct((1, IMAGES, CHAN,...  77.7 us
    unnamed x2, local copies, waits for them, and re-layouts  2.43 us

profile of v8, /device:TPU:1, one launch (start us, length us, event | category | flops | bytes accessed | tf_op | source)
XLA Modules:
  0.0 80.7 jit_solution(1949214891790865770)
XLA Ops:
  0.6 77.7 %shard_map.158 = (f32[1,4,4,128]{3,2,1,0:T(4,128)}, f32[1,4]{1,0:T(1,128)}) custom-call(s32[1,2]{1,0:T(1,128)} %steps_ref.1, s32[4]{0:T(128)} %labels_ref.1, f32[1,4,4,128]{3,2,1,0:T(4,128)} %lat_ref.1, f32[4,4,128]{2,1,0:T(4,128)} %anchor_ref.1, f32[1,4,4,128]{3,2,1,0:T(4,128)} %noise_ref.1, f32[1,128]{1,0:T(1,128)} %constant.8.clone.freq_ref, ...), custom_call_target="tpu_custom_call" | custom-call | flops 6000000000 | bytes 8000000 | tf_op jit(solution)/shard_map/pallas_call | solution.py:426
  78.3 1.3 %copy.19 = f32[1,4,4,128]{3,2,1,0:T(4,128)} copy(f32[1,4,4,128]{3,2,1,0:T(4,128)} %get-tuple-element.4) | data formatting | bytes 16384
  79.6 1.1 %copy.20 = f32[1,4]{1,0:T(1,128)} copy(f32[1,4]{1,0:T(1,128)} %get-tuple-element.5) | data formatting | bytes 32

commit v9 on v8

--- a/solution.py
+++ b/solution.py
@@ -143,6 +143,43 @@
             zw[z] = packed[0:16].astype(BF16)
             zr[z] = packed[16:18]
 
+    pl.semaphore_wait(barrier, NZ - 1 + NX - 1 + NT - 1 + NT)
+
+    def prior_copy(k):
+        return remote(psrc, pr.at[tok], pr_send.at[k], pr_recv.at[tok], (after, k))
+
+    def prior_arrival(k):
+        return remote(psrc, pr.at[k], pr_send.at[k], pr_recv.at[k], (after, k))
+
+    def zw_copy(k):
+        return remote(zw.at[z], zw.at[z], zw_send.at[k], zw_recv.at[k], z_peer(k))
+
+    def zr_copy(k):
+        return remote(zr.at[z], zr.at[z], zr_send.at[k], zr_recv.at[k], z_peer(k))
+
+    def zo_copy(k):
+        return remote(zo.at[z], zo.at[z], zo_send.at[k], zo_recv.at[k], z_peer(k))
+
+    def wx_copy(k):
+        return remote(wx.at[x], wx.at[x], wx_send.at[k], wx_recv.at[k], x_peer(k))
+
+    def ox_copy(k):
+        return remote(wob.at[core, x], wob.at[core, x], ox_send.at[k], ox_recv.at[k], x_peer(k))
+
+    def mod_copy(k):
+        return remote(mod_s, mod_r.at[tok], mod_send.at[k], mod_recv.at[k], t_peer(k))
+
+    def att_copy(b, k):
+        there = lax.rem(tok + k, NT)
+        return remote(att_s.at[b, there], att_r.at[b, tok], att_send.at[b, k], att_recv.at[b, k], t_peer(k))
+
+    def start_w(k):
+        zw_copy(k).start()
+        zr_copy(k).start()
+
+    each(NZ, start_w)
+    each(NT, lambda k: prior_copy(k).start(), first=0)
+
     grid = lax.broadcasted_iota(jnp.int32, (SIDE, TOKENS), 1)
     line = lax.broadcasted_iota(jnp.int32, (SIDE, TOKENS), 0)
     chosen = [jnp.where(line == (grid >> 5), 1.0, 0.0), jnp.where(line == (grid & 31), 1.0, 0.0)]
@@ -160,44 +197,6 @@
                 po[CHUNK * i : CHUNK * i + CHUNK] = wide[:, 128 * k : 128 * k + 128]
 
     zo[z] = po[...].astype(BF16)
-    pl.semaphore_wait(barrier, NZ - 1 + NX - 1 + NT - 1 + NT)
-
-    def prior_copy(k):
-        return remote(psrc, pr.at[tok], pr_send.at[k], pr_recv.at[tok], (after, k))
-
-    def prior_arrival(k):
-        return remote(psrc, pr.at[k], pr_send.at[k], pr_recv.at[k], (after, k))
-
-    def zw_copy(k):
-        return remote(zw.at[z], zw.at[z], zw_send.at[k], zw_recv.at[k], z_peer(k))
-
-    def zr_copy(k):
-        return remote(zr.at[z], zr.at[z], zr_send.at[k], zr_recv.at[k], z_peer(k))
-
-    def zo_copy(k):
-        return remote(zo.at[z], zo.at[z], zo_send.at[k], zo_recv.at[k], z_peer(k))
-
-    def wx_copy(k):
-        return remote(wx.at[x], wx.at[x], wx_send.at[k], wx_recv.at[k], x_peer(k))
-
-    def ox_copy(k):
-        return remote(wob.at[core, x], wob.at[core, x], ox_send.at[k], ox_recv.at[k], x_peer(k))
-
-    def mod_copy(k):
-        return remote(mod_s, mod_r.at[tok], mod_send.at[k], mod_recv.at[k], t_peer(k))
-
-    def att_copy(b, k):
-        there = lax.rem(tok + k, NT)
-        return remote(att_s.at[b, there], att_r.at[b, tok], att_send.at[b, k], att_recv.at[b, k], t_peer(k))
-
-    each(NT, lambda k: prior_copy(k).start(), first=0)
-
-    def start_w(k):
-        zw_copy(k).start()
-        zr_copy(k).start()
-
-    each(NZ, start_w)
-
     t_from = jnp.full((1, 128), steps_ref[0, 0].astype(F32))
     t_to = jnp.full((1, 128), steps_ref[0, 1].astype(F32))
     phases = t_from * freq_ref[...]
@@ -242,6 +241,17 @@
     crosses = jnp.dot(crosses, xs[0:128], preferred_element_type=F32)
     crosses = (crosses[0:8] + crosses[8:16] + crosses[16:24])[0:CHAN]
 
+    def arrive_w(k):
+        zw_copy(k).wait()
+        zr_copy(k).wait()
+
+    each(NZ, arrive_w)
+    for i in range(NZ):
+        wf[18 * i : 18 * i + 16] = zw[i].astype(F32)
+        wf[18 * i + 16 : 18 * i + 18] = zr[i]
+    wx[x] = wf[...].astype(BF16)
+    each(NX, lambda k: wx_copy(k).start())
+    each(NZ, lambda k: zo_copy(k).start())
     each(NT, lambda k: mod_copy(k).wait())
     for source in range(NT):
         mod_t[source * 432 : source * 432 + 432] = jnp.transpose(mod_r[source])[0:432]
@@ -281,17 +291,6 @@
         invs[b] = lax.rsqrt(jnp.maximum(variance, 0.0) + 1e-06)
         xo[:, b * 128 : b * 128 + 128] = xs[:, pl.ds(pl.multiple_of(tok * 128, 128), 128)]
 
-    def arrive_w(k):
-        zw_copy(k).wait()
-        zr_copy(k).wait()
-
-    each(NZ, arrive_w)
-    each(NZ, lambda k: zo_copy(k).start())
-    for i in range(NZ):
-        wf[18 * i : 18 * i + 16] = zw[i].astype(F32)
-        wf[18 * i + 16 : 18 * i + 18] = zr[i]
-    wx[x] = wf[...].astype(BF16)
-    each(NX, lambda k: wx_copy(k).start())
     own[...] = jnp.dot(tcat[...], xo[...], preferred_element_type=F32)
     each(NX, lambda k: wx_copy(k).wait())
     folded = lax.dot_general(

time: 80.9 us -> 78.9 us (0.975)
  Pallas kernels: 77.7 us -> 75.7 us
    pallas_call x1, Pallas kernels: 77.7 us -> 75.7 us  [body(): pl.pallas_call(kernel, out_shape=(jax.ShapeDtypeStruct((1, IMAGES, CHAN,...]
where the time goes in v9:
time: 78.9 us; the launch traced here: 78.7 us
  Pallas kernels  75.7 us (96%)
  local copies, waits for them, and re-layouts  2.43 us (3%)
    pallas_call x1, Pallas kernels, body(): pl.pallas_call(kernel, out_shape=(jax.ShapeDtypeStruct((1, IMAGES, CHAN,...  75.7 us
    unnamed x2, local copies, waits for them, and re-layouts  2.43 us

profile of v9, /device:TPU:1, one launch (start us, length us, event | category | flops | bytes accessed | tf_op | source)
XLA Modules:
  0.0 78.7 jit_solution(15772212018187873965)
XLA Ops:
  0.6 75.7 %shard_map.158 = (f32[1,4,4,128]{3,2,1,0:T(4,128)}, f32[1,4]{1,0:T(1,128)}) custom-call(s32[1,2]{1,0:T(1,128)} %steps_ref.1, s32[4]{0:T(128)} %labels_ref.1, f32[1,4,4,128]{3,2,1,0:T(4,128)} %lat_ref.1, f32[4,4,128]{2,1,0:T(4,128)} %anchor_ref.1, f32[1,4,4,128]{3,2,1,0:T(4,128)} %noise_ref.1, f32[1,128]{1,0:T(1,128)} %constant.8.clone.freq_ref, ...), custom_call_target="tpu_custom_call" | custom-call | flops 6000000000 | bytes 8000000 | tf_op jit(solution)/shard_map/pallas_call | solution.py:425
  76.3 1.3 %copy.19 = f32[1,4,4,128]{3,2,1,0:T(4,128)} copy(f32[1,4,4,128]{3,2,1,0:T(4,128)} %get-tuple-element.4) | data formatting | bytes 16384
  77.6 1.1 %copy.20 = f32[1,4]{1,0:T(1,128)} copy(f32[1,4]{1,0:T(1,128)} %get-tuple-element.5) | data formatting | bytes 32
